TPU v7x, 32 devices: a whole 2x2x4 slice. The times are simulated.
32 devices in a mesh: bulk: 8 (over y, x, core), view: 4 (over z).
Axes of the slice: x: 2, y: 2, z: 4, core: 2. Of those that a mesh axis runs over, the one named last changes fastest.
Arguments:
- planes: bfloat16 [32, 512, 512], P('view', 'bulk'), may hold values from -6 to 6
- cand_index: int32 [8, 4, 8, 128], P('bulk', 'view'), may hold values from 0 to 2047
- recv_slot: int32 [8, 4, 8, 128], P('bulk', 'view'), may hold values from 0 to 1023
- recv_count: int32 [8, 4, 8], P('bulk', 'view'), may hold values from 1 to 128, as said below
Outputs:
- dog: bfloat16 [32, 512, 512], P(None, 'bulk', 'view')
- descriptors: float32 [8, 4, 1024, 128], P('bulk', 'view')
Inputs may be any that keep to these rules, and one draw needn't show every extreme that they name: `recv_count`: for each owner and view either every brick offers 128 accepted rows, or each brick has 16 to 64 accepted rows (at least 1); some owner and view accepts 128 from every brick.
All inputs are finite; a program needn't handle non-finite values.
Results may differ from a plain program's by a relative error of at most 0.0034.
Values may be sent and summed in bfloat16 or wider, within the bound.
No kernel may reach another device: no remote copies, remote signals or barrier semaphores. Data moves between devices by JAX's collectives and lax.ppermute only.
A program may use at most 64 MiB of HBM per device.

v0:
```python
import math

import jax
import jax.numpy as jnp
from jax import lax
from jax.sharding import PartitionSpec as P

RADIUS = 8
SLOTS = 1024


narrow_sigma = (1.0, 2.0, 2.0)
broad_sigma = (1.6, 3.2, 3.2)
contrast = 20.0
epsilon = 1e-06


def with_halo(block, sides, width):
    for axis, dim in sides:
        count = lax.axis_size(axis)
        forward = [(i, i + 1) for i in range(count - 1)]
        backward = [(target, source) for source, target in forward]
        low = lax.ppermute(
            lax.slice_in_dim(block, block.shape[dim] - width, None, axis=dim), axis, forward
        )
        high = lax.ppermute(lax.slice_in_dim(block, 0, width, axis=dim), axis, backward)
        block = jnp.concatenate([low, block, high], axis=dim)
    return block


def gauss_taps(sigma, radius):
    weights = [math.exp(-0.5 * (offset / sigma) ** 2) for offset in range(-radius, radius + 1)]
    scale_total = sum(weights)
    return [weight / scale_total for weight in weights]


def tap_table(radius):
    return [
        [gauss_taps(narrow_sigma[along], radius), gauss_taps(broad_sigma[along], radius)]
        for along in range(3)
    ]


def smooth(fields, weights, along, radius):
    length = fields.shape[along] - 2 * radius
    total = None
    for offset in range(2 * radius + 1):
        shifted = lax.slice_in_dim(fields, offset, offset + length, axis=along).astype(jnp.float32)
        term = weights[:, offset].reshape((2,) + (1,) * (fields.ndim - 1)) * shifted
        total = term if total is None else total + term
    return total


def depth_pass(brick, table):
    padded = jnp.pad(brick, ((RADIUS, RADIUS), (0, 0), (0, 0)))
    return smooth(padded[None], table[0], 1, RADIUS)


def local(planes, cand_index, recv_slot, recv_count):
    table = jnp.asarray(tap_table(RADIUS), jnp.float32)
    views = lax.axis_size("view")
    zlocal, rows_y, width_x = planes.shape
    cells_x = width_x // views
    main = planes.reshape(zlocal, rows_y, views, cells_x)
    arrived = lax.all_to_all(main, "view", split_axis=2, concat_axis=0, tiled=True)
    brick = arrived.reshape(arrived.shape[0], rows_y, arrived.shape[3])
    fields = depth_pass(brick, table)
    fields = with_halo(fields, (("bulk", 2),), RADIUS)
    fields = smooth(fields, table[1], 2, RADIUS)
    fields = with_halo(fields, (("view", 3),), RADIUS)
    fields = smooth(fields, table[2], 3, RADIUS)
    dog = (contrast * (fields[0] - fields[1])).astype(jnp.bfloat16)
    owners = cand_index.shape[2]
    offered = cand_index.shape[3]
    flat_dog = dog.reshape(-1, dog.shape[2])
    chosen = jnp.take(flat_dog, cand_index.reshape(-1), axis=0).reshape(
        owners, offered, dog.shape[2]
    )
    slot_ids = recv_slot.reshape(-1)
    keep = (
        jnp.arange(offered, dtype=jnp.int32)[None, :] < recv_count.reshape(owners)[:, None]
    ).reshape(-1)
    block_size = min(SLOTS, 256)
    received = lax.all_to_all(chosen, "bulk", split_axis=0, concat_axis=0, tiled=True)
    flat_rows = received.reshape(-1, received.shape[2])
    outputs = []
    for start in range(0, SLOTS, block_size):
        targets = start + jnp.arange(block_size, dtype=jnp.int32)
        onehot = ((slot_ids[None, :] == targets[:, None]) & keep[None, :]).astype(jnp.bfloat16)
        outputs.append(jnp.dot(onehot, flat_rows, preferred_element_type=jnp.float32))
    summed = jnp.concatenate(outputs, axis=0)
    descriptors = summed / jnp.sqrt(jnp.mean(summed * summed, axis=-1, keepdims=True) + epsilon)
    return (dog, descriptors.reshape(1, 1, SLOTS, summed.shape[1]))


def solution(mesh):
    in_specs = (
        P("view", "bulk", None),
        P("bulk", "view", None, None),
        P("bulk", "view", None, None),
        P("bulk", "view", None),
    )
    out_specs = (P(None, "bulk", "view"), P("bulk", "view", None, None))
    return jax.shard_map(local, mesh=mesh, in_specs=in_specs, out_specs=out_specs, check_vma=False)
```

profile of v0, /device:TPU:0, one launch (start us, length us, event | category | flops | bytes accessed | tf_op | source)
XLA Modules:
  0.0 116.1 jit_solution(7466060875311435086)
XLA Ops:
  0.6 0.0 copy-start
  0.6 0.0 copy-start.23
  0.7 0.0 copy-start.3
  0.7 1.0 copy-done
  1.7 0.9 copy_bitcast_fusion
  2.6 6.3 %all-to-all-start = ((bf16[8,64,4,128]{3,1,0,2:T(8,128)(2,1)}), bf16[8,64,4,128]{3,1,0,2:T(8,128)(2,1)S(1)}, u32[]{:S(2)}, u32[]{:S(2)}) async-start(bf16[8,64,4,128]{3,1,0,2:T(8,128)(2,1)} %copy_bitcast_fusion), calls=%async_computation | async-start | bytes 1048576 | tf_op jit(solution)/shard_map/all_to_all | solution.py:65
  8.9 0.0 copy-done.23
  8.9 0.1 fusion.135
  9.0 0.0 copy-done.3
  9.0 14.4 %all-to-all-done = bf16[8,64,4,128]{3,1,0,2:T(8,128)(2,1)S(1)} async-done(((bf16[8,64,4,128]{3,1,0,2:T(8,128)(2,1)}), bf16[8,64,4,128]{3,1,0,2:T(8,128)(2,1)S(1)}, u32[]{:S(2)}, u32[]{:S(2)}) %all-to-all-start) | async-done | bytes 524320 | tf_op jit(solution)/shard_map/all_to_all | solution.py:65
  23.4 0.1 pad_bitcast_fusion
  23.5 0.0 copy-start.13
  23.5 0.0 copy-start.14
  23.6 0.0 copy-start.15
  23.6 0.0 copy-start.16
  23.6 0.0 copy-start.17
  23.6 0.0 copy-start.18
  23.6 0.0 copy-start.19
  23.6 0.0 copy-start.20
  23.6 0.0 copy-start.21
  23.6 5.5 %fusion.122 = (f32[32,64,128]{2,1,0:T(8,128)S(1)}, f32[32,64,128]{2,1,0:T(8,128)S(1)}, f32[32,64,128]{2,1,0:T(8,128)}, f32[32,64,128]{2,1,0:T(8,128)}, f32[32,64...) fusion(bf16[1,48,64,128]{3,2,1,0:T(8,128)(2,1)S(1)} %pad_bitcas, ...), kind=kLoop, calls=%fused_computation.204 | loop fusion | flops 4456448 | bytes 26738688 | tf_op jit(solution)/shard_map/mul | solution.py:49
  29.2 0.0 copy-done.13
  29.2 0.0 copy-done.14
  29.3 0.0 copy-start.4
  29.3 0.0 copy-start.5
  29.3 0.0 copy-start.6
  29.3 0.0 copy-start.7
  29.3 0.0 copy-start.8
  29.3 0.0 copy-start.9
  29.3 0.0 copy-start.10
  29.4 0.0 copy-start.11
  29.4 0.0 copy-start.12
  29.4 6.7 %multiply_add_fusion = f32[2,32,64,128]{3,2,1,0:T(8,128)S(1)} fusion(f32[32,64,128]{2,1,0:T(8,128)S(1)} %get-tuple-element.11, f32[32,64,128]{2,1,0:T(8,128)} %get-tuple-element.12, f32[32,64,128]{2,1,0:T(8,128)} %get-tuple-element.13, f32[32,64,128]{2,1,0:T(8,128)} %get-tuple-element.14, f32[32,64,128]{2,1,0:T(8,128)} %get-tuple-element.15, ...), kind=kLoop, calls=%fused_computation.153 | loop fusion | flops 17301504 | bytes 19923016 | tf_op jit(solution)/shard_map/add | solution.py:50
  36.2 1.3 %collective-permute-start = (f32[2,32,8,128]{3,2,1,0:T(8,128)S(1)}, f32[2,32,8,128]{3,2,1,0:T(8,128)S(1)}, u32[]{:S(2)}, u32[]{:S(2)}) collective-permute-start(f32[2,32,8,128]{3,2,1,0:T(8,128)S(1)} %get-tuple-element.8), channel_id=1, source_target_pairs={{0,4},{4,8},{8,12},{12,16},{16,20},{20,24},{24,28},{1,5},{5,9},{9,... | collective-permute-start | bytes 786440 | tf_op jit(solution)/shard_map/ppermute | solution.py:23
  37.5 1.3 %collective-permute-start.1 = (f32[2,32,8,128]{3,2,1,0:T(8,128)S(1)}, f32[2,32,8,128]{3,2,1,0:T(8,128)S(1)}, u32[]{:S(2)}, u32[]{:S(2)}) collective-permute-start(f32[2,32,8,128]{3,2,1,0:T(8,128)S(1)} %get-tuple-element.9), channel_id=1, source_target_pairs={{4,0},{8,4},{12,8},{16,12},{20,16},{24,20},{28,24},{5,1},{9,5},{13... | collective-permute-start | bytes 786440 | tf_op jit(solution)/shard_map/ppermute | solution.py:26
  38.8 0.0 collective-permute-done
  38.8 3.8 %collective-permute-done.1 = f32[2,32,8,128]{3,2,1,0:T(8,128)S(1)} collective-permute-done((f32[2,32,8,128]{3,2,1,0:T(8,128)S(1)}, f32[2,32,8,128]{3,2,1,0:T(8,128)S(1)}, u32[]{:S(2)}, u32[]{:S(2)}) %collective-permute-start.1) | collective-permute-done | bytes 262176 | tf_op jit(solution)/shard_map/ppermute | solution.py:26
  42.6 0.0 copy-done.4
  42.6 0.0 copy-done.6
  42.7 5.0 %fusion.3 = f32[2,32,64,128]{3,2,1,0:T(8,128)S(1)} fusion(f32[2,32,64,128]{3,2,1,0:T(8,128)S(1)} %multiply_add_fusion, f32[2,32,8,128]{3,2,1,0:T(8,128)S(1)} %collective-permute-done.1, f32[2,32,8,128]{3,2,1,0:T(8,128)S(1)} %collective-permute-done, f32[2]{0:T(128)S(1)} %copy-done.4, f32[2]{0:T(128)S(1)} %copy-done.12, f32[2]{0:T(128)S(1)} %copy-done.11, ...), kind=kLoop, calls=%fused_computation.60 | loop fusion | flops 25690112 | bytes 4718664 | tf_op jit(solution)/shard_map/add | solution.py:50
  47.7 2.7 %fusion.136 = (f32[2,32,64,8]{3,2,1,0:T(8,128)}, f32[2,32,64,8]{3,2,1,0:T(8,128)}) fusion(f32[2,32,64,128]{3,2,1,0:T(8,128)S(1)} %fusion.3), kind=kLoop, calls=%fused_computation.230 | loop fusion | bytes 524288 | tf_op jit(solution)/shard_map/slice | solution.py:24
  50.4 2.2 %copy.48 = f32[2,32,64,8]{2,3,1,0:T(8,128)S(1)} copy(f32[2,32,64,8]{3,2,1,0:T(8,128)} %get-tuple-element.6) | data formatting | bytes 262144 | tf_op jit(solution)/shard_map/slice | solution.py:24
  52.6 1.3 %collective-permute-start.2 = (f32[2,32,64,8]{2,3,1,0:T(8,128)S(1)}, f32[2,32,64,8]{2,3,1,0:T(8,128)S(1)}, u32[]{:S(2)}, u32[]{:S(2)}) collective-permute-start(f32[2,32,64,8]{2,3,1,0:T(8,128)S(1)} %copy.48), channel_id=1, source_target_pairs={{0,1},{1,2},{2,3},{4,5},{5,6},{6,7},{8,9},{9,10},{10,11},{12,13},{... | collective-permute-start | bytes 393224 | tf_op jit(solution)/shard_map/ppermute | solution.py:23
  53.9 2.2 %copy.50 = f32[2,32,64,8]{2,3,1,0:T(8,128)S(1)} copy(f32[2,32,64,8]{3,2,1,0:T(8,128)} %get-tuple-element.7) | data formatting | bytes 262144 | tf_op jit(solution)/shard_map/slice | solution.py:26
  56.1 1.3 %collective-permute-start.3 = (f32[2,32,64,8]{2,3,1,0:T(8,128)S(1)}, f32[2,32,64,8]{2,3,1,0:T(8,128)}, u32[]{:S(2)}, u32[]{:S(2)}) collective-permute-start(f32[2,32,64,8]{2,3,1,0:T(8,128)S(1)} %copy.50), channel_id=1, source_target_pairs={{1,0},{2,1},{3,2},{5,4},{6,5},{7,6},{9,8},{10,9},{11,10},{13,12},{... | collective-permute-start | bytes 393224 | tf_op jit(solution)/shard_map/ppermute | solution.py:26
  57.4 0.4 collective-permute-done.2
  57.8 2.0 %copy.49 = f32[2,32,64,8]{3,2,1,0:T(8,128)} copy(f32[2,32,64,8]{2,3,1,0:T(8,128)S(1)} %collective-permute-done.2) | data formatting | bytes 262144 | tf_op jit(solution)/shard_map/ppermute | solution.py:23
  59.7 4.7 %collective-permute-done.3 = f32[2,32,64,8]{2,3,1,0:T(8,128)} collective-permute-done((f32[2,32,64,8]{2,3,1,0:T(8,128)S(1)}, f32[2,32,64,8]{2,3,1,0:T(8,128)}, u32[]{:S(2)}, u32[]{:S(2)}) %collective-permute-start.3) | collective-permute-done | bytes 131104 | tf_op jit(solution)/shard_map/ppermute | solution.py:26
  64.4 2.9 %copy.51 = f32[2,32,64,8]{3,2,1,0:T(8,128)} copy(f32[2,32,64,8]{2,3,1,0:T(8,128)} %collective-permute-done.3) | data formatting | bytes 262144 | tf_op jit(solution)/shard_map/ppermute | solution.py:26
  67.4 23.9 %fusion.47 = f32[2,32,64,128]{3,2,1,0:T(8,128)S(1)} fusion(f32[2,32,64,128]{3,2,1,0:T(8,128)S(1)} %fusion.3, f32[2,32,64,8]{3,2,1,0:T(8,128)} %copy.51, f32[2,32,64,8]{3,2,1,0:T(8,128)} %copy.49, f32[2]{0:T(128)S(1)} %copy-done.4, f32[2]{0:T(128)S(1)} %copy-done.12, f32[2]{0:T(128)S(1)} %copy-done.11, f32[2]{0:T(128)S(1)} %copy-done.10, f32[2]{0:T(128)S(1)} %copy-done.9, ...), kind=kLoop, calls=%fused_computation.104 | loop fusion | flops 25690112 | bytes 4456520 | tf_op jit(solution)/shard_map/add | solution.py:50
  91.3 1.4 %copy-done.1 = f32[2,32,64,128]{3,2,1,0:T(8,128)} copy-done((f32[2,32,64,128]{3,2,1,0:T(8,128)}, f32[2,32,64,128]{3,2,1,0:T(8,128)S(1)}, u32[]{:S(2)}) %copy-start.1) | copy-done | bytes 2097176
  92.7 0.2 fusion.93
  92.9 3.2 %gather_fusion = bf16[1024,128]{1,0:T(8,128)(2,1)S(1)} fusion(bf16[2048,128]{1,0:T(8,128)(2,1)S(1)} %bitcast.120, s32[1024]{0:T(1024)S(1)} %broadcast_clamp_fusion), kind=kCustom, calls=%fused_computation | custom fusion | bytes 528384 | tf_op jit(solution)/shard_map/jit(_take)/gather | solution.py:76
  96.1 0.0 copy-start.22
  96.1 0.9 broadcast_select_fusion
  97.0 9.4 %all-to-all-start.1 = ((bf16[8,128,128]{2,1,0:T(8,128)(2,1)}), bf16[8,128,128]{2,1,0:T(8,128)(2,1)S(1)}, u32[]{:S(2)}, u32[]{:S(2)}) async-start(bf16[8,128,128]{2,1,0:T(8,128)(2,1)} %broadcast_select_fusion), calls=%async_computation.1 | async-start | bytes 524288 | tf_op jit(solution)/shard_map/all_to_all | solution.py:84
  106.4 1.0 fusion.142
  107.4 5.9 %all-to-all-done.1 = bf16[8,128,128]{2,1,0:T(8,128)(2,1)S(1)} async-done(((bf16[8,128,128]{2,1,0:T(8,128)(2,1)}), bf16[8,128,128]{2,1,0:T(8,128)(2,1)S(1)}, u32[]{:S(2)}, u32[]{:S(2)}) %all-to-all-start.1) | async-done | bytes 262176 | tf_op jit(solution)/shard_map/all_to_all | solution.py:84
  113.4 0.3 fusion.95
  113.7 0.4 fusion.100
  114.1 0.4 fusion.103
  114.4 0.4 fusion.97
  114.8 0.2 fusion.123
  115.1 1.0 maximum_divide_fusion
  (26 shorter events, 0.1 us)
Async XLA Ops:
  0.6 1.0 copy-start
  0.6 8.3 %copy-start.23 = (s32[1,1,8]{2,1,0:T(1,128)S(1)}, s32[1,1,8]{2,1,0:T(1,128)}, u32[]{:S(2)}) copy-start(s32[1,1,8]{2,1,0:T(1,128)} %param.8) | copy-start | bytes 100
  0.7 8.4 %copy-start.3 = (s32[1,1,8,128]{3,2,1,0:T(8,128)S(1)}, s32[1,1,8,128]{3,2,1,0:T(8,128)}, u32[]{:S(2)}) copy-start(s32[1,1,8,128]{3,2,1,0:T(8,128)} %param.6) | copy-start | bytes 12292
  2.6 20.8 %all-to-all-start = ((bf16[8,64,4,128]{3,1,0,2:T(8,128)(2,1)}), bf16[8,64,4,128]{3,1,0,2:T(8,128)(2,1)S(1)}, u32[]{:S(2)}, u32[]{:S(2)}) async-start(bf16[8,64,4,128]{3,1,0,2:T(8,128)(2,1)} %copy_bitcast_fusion), calls=%async_computation | async-start | bytes 1048576 | tf_op jit(solution)/shard_map/all_to_all | solution.py:65
  23.5 5.7 %copy-start.13 = (f32[2]{0:T(128)S(1)}, f32[2]{0:T(128)}, u32[]{:S(2)}) copy-start(f32[2]{0:T(128)} %constant.53) | copy-start | bytes 28
  23.5 5.6 %copy-start.14 = (f32[2]{0:T(128)S(1)}, f32[2]{0:T(128)}, u32[]{:S(2)}) copy-start(f32[2]{0:T(128)} %constant.55) | copy-start | bytes 28
  23.6 5.6 %copy-start.15 = (f32[2]{0:T(128)S(1)}, f32[2]{0:T(128)}, u32[]{:S(2)}) copy-start(f32[2]{0:T(128)} %constant.57) | copy-start | bytes 28
  23.6 5.6 %copy-start.16 = (f32[2]{0:T(128)S(1)}, f32[2]{0:T(128)}, u32[]{:S(2)}) copy-start(f32[2]{0:T(128)} %constant.59) | copy-start | bytes 28
  23.6 5.6 %copy-start.17 = (f32[2]{0:T(128)S(1)}, f32[2]{0:T(128)}, u32[]{:S(2)}) copy-start(f32[2]{0:T(128)} %constant.61) | copy-start | bytes 28
  23.6 5.6 %copy-start.18 = (f32[2]{0:T(128)S(1)}, f32[2]{0:T(128)}, u32[]{:S(2)}) copy-start(f32[2]{0:T(128)} %constant.63) | copy-start | bytes 28
  23.6 5.6 %copy-start.19 = (f32[2]{0:T(128)S(1)}, f32[2]{0:T(128)}, u32[]{:S(2)}) copy-start(f32[2]{0:T(128)} %constant.65) | copy-start | bytes 28
  23.6 5.6 %copy-start.20 = (f32[2]{0:T(128)S(1)}, f32[2]{0:T(128)}, u32[]{:S(2)}) copy-start(f32[2]{0:T(128)} %constant.67) | copy-start | bytes 28
  23.6 5.6 %copy-start.21 = (f32[2]{0:T(128)S(1)}, f32[2]{0:T(128)}, u32[]{:S(2)}) copy-start(f32[2]{0:T(128)} %constant.69) | copy-start | bytes 28
  29.3 13.3 %copy-start.4 = (f32[2]{0:T(128)S(1)}, f32[2]{0:T(128)}, u32[]{:S(2)}) copy-start(f32[2]{0:T(128)} %constant.101) | copy-start | bytes 28
  29.3 13.3 %copy-start.5 = (f32[2]{0:T(128)S(1)}, f32[2]{0:T(128)}, u32[]{:S(2)}) copy-start(f32[2]{0:T(128)} %constant.45) | copy-start | bytes 28
  29.3 13.3 %copy-start.6 = (f32[2]{0:T(128)S(1)}, f32[2]{0:T(128)}, u32[]{:S(2)}) copy-start(f32[2]{0:T(128)} %constant.87) | copy-start | bytes 28
  29.3 13.3 %copy-start.7 = (f32[2]{0:T(128)S(1)}, f32[2]{0:T(128)}, u32[]{:S(2)}) copy-start(f32[2]{0:T(128)} %constant.89) | copy-start | bytes 28
  29.3 13.3 %copy-start.8 = (f32[2]{0:T(128)S(1)}, f32[2]{0:T(128)}, u32[]{:S(2)}) copy-start(f32[2]{0:T(128)} %constant.91) | copy-start | bytes 28
  29.3 13.3 %copy-start.9 = (f32[2]{0:T(128)S(1)}, f32[2]{0:T(128)}, u32[]{:S(2)}) copy-start(f32[2]{0:T(128)} %constant.93) | copy-start | bytes 28
  29.3 13.3 %copy-start.10 = (f32[2]{0:T(128)S(1)}, f32[2]{0:T(128)}, u32[]{:S(2)}) copy-start(f32[2]{0:T(128)} %constant.95) | copy-start | bytes 28
  29.4 13.3 %copy-start.11 = (f32[2]{0:T(128)S(1)}, f32[2]{0:T(128)}, u32[]{:S(2)}) copy-start(f32[2]{0:T(128)} %constant.97) | copy-start | bytes 28
  29.4 13.3 %copy-start.12 = (f32[2]{0:T(128)S(1)}, f32[2]{0:T(128)}, u32[]{:S(2)}) copy-start(f32[2]{0:T(128)} %constant.99) | copy-start | bytes 28
  36.2 2.6 %collective-permute-start = (f32[2,32,8,128]{3,2,1,0:T(8,128)S(1)}, f32[2,32,8,128]{3,2,1,0:T(8,128)S(1)}, u32[]{:S(2)}, u32[]{:S(2)}) collective-permute-start(f32[2,32,8,128]{3,2,1,0:T(8,128)S(1)} %get-tuple-element.8), channel_id=1, source_target_pairs={{0,4},{4,8},{8,12},{12,16},{16,20},{20,24},{24,28},{1,5},{5,9},{9,... | collective-permute-start | bytes 786440 | tf_op jit(solution)/shard_map/ppermute | solution.py:23
  37.5 5.1 %collective-permute-start.1 = (f32[2,32,8,128]{3,2,1,0:T(8,128)S(1)}, f32[2,32,8,128]{3,2,1,0:T(8,128)S(1)}, u32[]{:S(2)}, u32[]{:S(2)}) collective-permute-start(f32[2,32,8,128]{3,2,1,0:T(8,128)S(1)} %get-tuple-element.9), channel_id=1, source_target_pairs={{4,0},{8,4},{12,8},{16,12},{20,16},{24,20},{28,24},{5,1},{9,5},{13... | collective-permute-start | bytes 786440 | tf_op jit(solution)/shard_map/ppermute | solution.py:26
  52.6 5.2 %collective-permute-start.2 = (f32[2,32,64,8]{2,3,1,0:T(8,128)S(1)}, f32[2,32,64,8]{2,3,1,0:T(8,128)S(1)}, u32[]{:S(2)}, u32[]{:S(2)}) collective-permute-start(f32[2,32,64,8]{2,3,1,0:T(8,128)S(1)} %copy.48), channel_id=1, source_target_pairs={{0,1},{1,2},{2,3},{4,5},{5,6},{6,7},{8,9},{9,10},{10,11},{12,13},{... | collective-permute-start | bytes 393224 | tf_op jit(solution)/shard_map/ppermute | solution.py:23
  56.1 8.4 %collective-permute-start.3 = (f32[2,32,64,8]{2,3,1,0:T(8,128)S(1)}, f32[2,32,64,8]{2,3,1,0:T(8,128)}, u32[]{:S(2)}, u32[]{:S(2)}) collective-permute-start(f32[2,32,64,8]{2,3,1,0:T(8,128)S(1)} %copy.50), channel_id=1, source_target_pairs={{1,0},{2,1},{3,2},{5,4},{6,5},{7,6},{9,8},{10,9},{11,10},{13,12},{... | collective-permute-start | bytes 393224 | tf_op jit(solution)/shard_map/ppermute | solution.py:26
  91.3 1.4 %copy-start.1 = (f32[2,32,64,128]{3,2,1,0:T(8,128)}, f32[2,32,64,128]{3,2,1,0:T(8,128)S(1)}, u32[]{:S(2)}) copy-start(f32[2,32,64,128]{3,2,1,0:T(8,128)S(1)} %fusion.47) | copy-start | bytes 6291460
  92.9 13.5 %copy-start.2 = (f32[2,32,64,128]{3,2,1,0:T(8,128)S(1)}, f32[2,32,64,128]{3,2,1,0:T(8,128)}, u32[]{:S(2)}) copy-start(f32[2,32,64,128]{3,2,1,0:T(8,128)} %copy-done.1) | copy-start | bytes 6291460
  96.1 17.3 %copy-start.22 = (s32[1,1,8,128]{3,2,1,0:T(8,128)S(1)}, s32[1,1,8,128]{3,2,1,0:T(8,128)}, u32[]{:S(2)}) copy-start(s32[1,1,8,128]{3,2,1,0:T(8,128)} %param.7) | copy-start | bytes 12292
  97.0 16.3 %all-to-all-start.1 = ((bf16[8,128,128]{2,1,0:T(8,128)(2,1)}), bf16[8,128,128]{2,1,0:T(8,128)(2,1)S(1)}, u32[]{:S(2)}, u32[]{:S(2)}) async-start(bf16[8,128,128]{2,1,0:T(8,128)(2,1)} %broadcast_select_fusion), calls=%async_computation.1 | async-start | bytes 524288 | tf_op jit(solution)/shard_map/all_to_all | solution.py:84
where the time goes:
time: 117 us; the launch traced here: 116 us
  other arithmetic  44.6 us (38%)
  waiting for transfers between devices  29.2 us (25%)
  starting transfers between devices  20.9 us (18%)
  local copies, waits for them, and re-layouts  18.7 us (16%)
  matrix products  1.44 us (1%)
    add x3, other arithmetic, smooth(): total = term if total is None else total + term  35.6 us
    all_to_all x1, waiting for transfers between devices, local(): lax.all_to_all(main, 'view', split_axis=2, concat_axis=0, tiled=True)  14.4 us
    all_to_all x1, starting transfers between devices, local(): lax.all_to_all(chosen, 'bulk', split_axis=0, concat_axis=0, tiled=True)  9.4 us
    ppermute x2, waiting for transfers between devices, with_halo(): lax.ppermute(lax.slice_in_dim(block, 0, width, axis=dim), axis, backward)  8.54 us
    all_to_all x1, starting transfers between devices, local(): lax.all_to_all(main, 'view', split_axis=2, concat_axis=0, tiled=True)  6.32 us
    all_to_all x1, waiting for transfers between devices, local(): lax.all_to_all(chosen, 'bulk', split_axis=0, concat_axis=0, tiled=True)  5.94 us
    mul x1, other arithmetic, smooth(): term = weights[:, offset].reshape((2,) + (1,) * (fields.ndim - 1)) * shifted  5.54 us
    slice x3, local copies, waits for them, and re-layouts, with_halo(): lax.slice_in_dim(block, block.shape[dim] - width, None, axis=dim)  4.93 us
  transfers between devices with their start and end apart: 6, of which 5 were waited for; matrix products, arithmetic and copies ran while one was open for 4% of the time, Pallas kernels for 0%

commit v1 on v0

v1 whole, which is shorter than its diff:
```python
import math

import jax
import jax.numpy as jnp
import numpy as np
from jax import lax
from jax.experimental import pallas as pl
from jax.experimental.pallas import tpu as pltpu
from jax.sharding import PartitionSpec as P

RADIUS = 8
SLOTS = 1024
LANES = 128

narrow_sigma = (1.0, 2.0, 2.0)
broad_sigma = (1.6, 3.2, 3.2)
contrast = 20.0
epsilon = 1e-06

F32 = jnp.float32
BF16 = jnp.bfloat16


def gauss_taps(sigma, radius):
    weights = [math.exp(-0.5 * (offset / sigma) ** 2) for offset in range(-radius, radius + 1)]
    scale_total = sum(weights)
    return [weight / scale_total for weight in weights]


def taps(along):
    return [
        np.asarray(gauss_taps(sigma[along], RADIUS), np.float32)
        for sigma in (narrow_sigma, broad_sigma)
    ]


def split_bf16(array):
    high = array.astype(jnp.bfloat16)
    low = (array - high.astype(np.float32)).astype(jnp.bfloat16)
    return high, low


def band(where_in, where_out, tap):
    offset = np.asarray(where_in)[:, None] - np.asarray(where_out)[None, :] + RADIUS
    inside = (offset >= 0) & (offset <= 2 * RADIUS)
    return np.where(inside, tap[np.clip(offset, 0, 2 * RADIUS)], 0).astype(np.float32)


def x_weights(lane_groups):
    outs = np.arange(LANES)
    margin = list(range(-RADIUS, 0)) + list(range(LANES, LANES + RADIUS))
    both = [
        np.concatenate([band(outs, outs, tap), np.tile(band(margin, outs, tap), (lane_groups, 1))])
        for tap in taps(2)
    ]
    return np.stack(split_bf16(np.concatenate(both, axis=1)))


def y_weights(rows):
    low_edge, high_edge = list(range(RADIUS)), list(range(rows - RADIUS, rows))
    low_halo, high_halo = list(range(-RADIUS, 0)), list(range(rows, rows + RADIUS))
    interior = list(range(RADIUS, rows - RADIUS))
    orders = (
        high_edge + low_edge + high_halo + low_halo + interior,
        low_edge + high_edge + low_halo + high_halo + interior,
    )
    result = []
    for order in orders:
        fields = []
        for tap in taps(1):
            high, low = split_bf16(band(order, np.arange(rows), tap).T)
            wide = np.concatenate([high, low, high], axis=1)
            pad = -wide.shape[1] % LANES
            fields.append(np.pad(wide, ((0, 0), (0, pad))))
        result.append(np.stack(fields))
    return np.stack(result)


def edge_rows(zlocal):
    return -(-(zlocal + 1) * RADIUS // 16) * 16


def pack_kernel(planes_ref, *outs):
    views = len(outs) // 2
    edges, inner = outs[:views], outs[views:]
    zlocal, rows = planes_ref.shape[:2]
    me = lax.axis_index("view")
    odd = lax.axis_index("bulk") % 2 == 1
    lane = lax.broadcasted_iota(jnp.int32, (rows, LANES), 1)
    for k in range(views):
        dest = me ^ k

        def tile(z, which):
            return planes_ref[z, :, pl.ds(pl.multiple_of(which * LANES, LANES), LANES)].astype(F32)

        left = jnp.maximum(dest - 1, 0)
        right = jnp.minimum(dest + 1, views - 1)
        lowest = jnp.where(dest > 0, LANES - RADIUS, LANES)
        highest = jnp.where(dest < views - 1, RADIUS, 0)
        groups = []
        packed = jnp.zeros((rows, LANES), F32)
        for z in range(zlocal):
            margin = jnp.where(
                lane < highest, tile(z, right), jnp.where(lane >= lowest, tile(z, left), 0.0)
            )
            packed = packed + pltpu.roll(margin, (2 * RADIUS * z + RADIUS) % LANES, 1)
            groups.append(tile(z, dest))
        groups.append(packed)
        low = jnp.concatenate([g[:RADIUS] for g in groups], axis=0)
        high = jnp.concatenate([g[rows - RADIUS :] for g in groups], axis=0)
        pad = edges[k].shape[1] - low.shape[0]
        if pad:
            fill = jnp.zeros((pad, LANES), F32)
            low = jnp.concatenate([low, fill], axis=0)
            high = jnp.concatenate([high, fill], axis=0)
        edges[k][0] = jnp.where(odd, low, high).astype(BF16)
        edges[k][1] = jnp.where(odd, high, low).astype(BF16)
        for g, group in enumerate(groups):
            inner[k][g] = group[RADIUS : rows - RADIUS].astype(BF16)


def gather_edges_kernel(*refs):
    views = len(refs) - 2
    for k in range(views):
        for part in range(2):
            refs[views + part][k] = refs[k][part]


def filter_kernel(views, owners, *refs):
    edges = refs[:views]
    inner = refs[views : 2 * views]
    halo = refs[2 * views : 2 * views + 2]
    wx_ref, wy_ref, index_ref = refs[2 * views + 2 : 2 * views + 5]
    dog_ref = refs[2 * views + 5]
    chosen = refs[2 * views + 6 : 2 * views + 6 + owners]
    fields = refs[2 * views + 6 + owners :]
    planes_z, rows = dog_ref.shape[:2]
    zlocal = planes_z // views
    staged_rows = rows + 2 * RADIUS
    me = lax.axis_index("view")
    brick = lax.axis_index("bulk")
    parity = brick % 2

    def pieces(k):
        small = [edges[k][0], edges[k][1], halo[0][k], halo[1][k]]
        return [s.astype(F32) for s in small]

    small = [pieces(k) for k in range(views)]

    def rows_of(k, g):
        top = jnp.concatenate([s[g * RADIUS : (g + 1) * RADIUS] for s in small[k]], axis=0)
        return jnp.concatenate([top.astype(BF16), inner[k][g]], axis=0)

    margins = jnp.concatenate([rows_of(k, zlocal) for k in range(views)], axis=0)
    group = lax.broadcasted_iota(jnp.int32, (LANES, 2 * LANES), 0) // (2 * RADIUS)

    def x_pass(z):
        main = jnp.concatenate([rows_of(k, z) for k in range(views)], axis=0)
        operand = jnp.concatenate([main, margins], axis=1)
        total = None
        for part in range(2):
            margin_w = jnp.where(group == z, wx_ref[part, LANES:].astype(F32), 0.0).astype(BF16)
            weight = jnp.concatenate([wx_ref[part, :LANES], margin_w], axis=0)
            term = jnp.dot(operand, weight, preferred_element_type=F32)
            total = term if total is None else total + term
        return total

    wy = [wy_ref[parity, f] for f in range(2)]
    depth = wy[0].shape[1]
    fill = depth - 3 * staged_rows
    for z in range(0, zlocal, 2):
        pair = [x_pass(z), x_pass(z + 1)]
        for k in range(views):
            at = (me ^ k) * zlocal + z
            for f in range(2):
                data = jnp.concatenate(
                    [
                        p[k * staged_rows : (k + 1) * staged_rows, f * LANES : (f + 1) * LANES]
                        for p in pair
                    ],
                    axis=1,
                )
                high = data.astype(BF16)
                low = (data - high.astype(F32)).astype(BF16)
                parts = [high, high, low]
                if fill:
                    parts.append(jnp.zeros((fill, 2 * LANES), BF16))
                out = jnp.dot(wy[f], jnp.concatenate(parts, axis=0), preferred_element_type=F32)
                fields[f][at] = out[:, :LANES]
                fields[f][at + 1] = out[:, LANES:]

    z_taps = taps(0)
    scale = (contrast, -contrast)
    tile_rows = 16

    def z_pass(step, carry):
        at = pl.ds(pl.multiple_of(step * tile_rows, tile_rows), tile_rows)
        data = [[fields[f][z, at, :] for z in range(planes_z)] for f in range(2)]
        for z in range(planes_z):
            total = None
            for f in range(2):
                for reach in range(RADIUS + 1):
                    weight = float(scale[f] * z_taps[f][RADIUS + reach])
                    sides = [data[f][q] for q in {z - reach, z + reach} if 0 <= q < planes_z]
                    if not sides:
                        continue
                    both = sides[0] if len(sides) == 1 else sides[0] + sides[1]
                    term = weight * both
                    total = term if total is None else total + term
            dog_ref[z, at, :] = total.astype(BF16)
        return carry

    lax.fori_loop(0, rows // tile_rows, z_pass, 0)

    flat = dog_ref[...].reshape(planes_z * rows, LANES)
    wanted = jnp.concatenate(
        [index_ref[pl.ds(brick ^ m, 1), :] for m in range(owners)], axis=0
    ).astype(F32)
    columns = jnp.transpose(wanted)
    offered = columns.shape[0]
    position = lax.broadcasted_iota(jnp.int32, (offered, planes_z * rows), 1).astype(F32)
    for m in range(owners):
        onehot = jnp.where(columns[:, m : m + 1] == position, 1.0, 0.0).astype(BF16)
        chosen[m][...] = jnp.dot(onehot, flat, preferred_element_type=F32).astype(BF16)


def merge_kernel(owners, *refs):
    rows = refs[:owners]
    slot_ref, count_ref, out_ref = refs[owners:]
    owner = lax.axis_index("bulk")
    slots = out_ref.shape[0]
    offered = slot_ref.shape[1]
    candidate = lax.broadcasted_iota(jnp.int32, (1, offered), 1)
    block = 256
    received = jnp.concatenate([r[...] for r in rows], axis=0)
    targets = []
    for m in range(owners):
        slot = slot_ref[pl.ds(owner ^ m, 1), :]
        targets.append(jnp.where(candidate < count_ref[0, owner ^ m], slot, -1))
    target = jnp.concatenate(targets, axis=1)
    for start in range(0, slots, block):
        position = start + lax.broadcasted_iota(jnp.int32, (block, owners * offered), 0)
        onehot = jnp.where(position == target, 1.0, 0.0).astype(BF16)
        summed = jnp.dot(onehot, received, preferred_element_type=F32)
        scale = lax.rsqrt(jnp.mean(summed * summed, axis=-1, keepdims=True) + epsilon)
        out_ref[start : start + block] = summed * scale


def swap(block, axis, distance):
    count = lax.axis_size(axis)
    return lax.ppermute(block, axis, [(i, i ^ distance) for i in range(count)])


def local(planes, cand_index, recv_slot, recv_count):
    views = lax.axis_size("view")
    bricks = lax.axis_size("bulk")
    zlocal, rows, width = planes.shape
    planes_z = zlocal * views
    owners, offered = cand_index.shape[2:]
    vmem = pl.BlockSpec(memory_space=pltpu.VMEM)
    smem = pl.BlockSpec(memory_space=pltpu.SMEM)
    params = pltpu.CompilerParams(vmem_limit_bytes=48 * 1024 * 1024)
    edge = jax.ShapeDtypeStruct((2, edge_rows(zlocal), LANES), BF16)
    body = jax.ShapeDtypeStruct((zlocal + 1, rows - 2 * RADIUS, LANES), BF16)
    halo = jax.ShapeDtypeStruct((views, edge_rows(zlocal), LANES), BF16)

    packed = pl.pallas_call(
        pack_kernel,
        out_shape=[edge] * views + [body] * views,
        in_specs=[vmem],
        out_specs=[vmem] * (2 * views),
        compiler_params=params,
    )(planes)
    edges = [packed[0]] + [swap(packed[k], "view", k) for k in range(views - 1, 0, -1)][::-1]
    inner = [packed[views]] + [
        swap(packed[views + k], "view", k) for k in range(views - 1, 0, -1)
    ][::-1]
    near, far = pl.pallas_call(
        gather_edges_kernel,
        out_shape=[halo] * 2,
        in_specs=[vmem] * views,
        out_specs=[vmem] * 2,
        compiler_params=params,
    )(*edges)
    far_pairs = [(i, i + 1) for i in range(1, bricks - 1, 2)]
    far_pairs = far_pairs + [(target, source) for source, target in far_pairs]
    near = swap(near, "bulk", 1)
    far = lax.ppermute(far, "bulk", far_pairs)

    dog, *chosen = pl.pallas_call(
        lambda *refs: filter_kernel(views, owners, *refs),
        out_shape=[jax.ShapeDtypeStruct((planes_z, rows, LANES), BF16)]
        + [jax.ShapeDtypeStruct((offered, LANES), BF16)] * owners,
        in_specs=[vmem] * (2 * views + 5),
        out_specs=[vmem] * (1 + owners),
        scratch_shapes=[pltpu.VMEM((planes_z, rows, LANES), F32)] * 2,
        compiler_params=params,
    )(
        *edges,
        *inner,
        near,
        far,
        jnp.asarray(x_weights(LANES // (2 * RADIUS))),
        jnp.asarray(y_weights(rows)),
        cand_index.reshape(owners, offered),
    )
    received = [chosen[0]] + [
        swap(chosen[m], "bulk", m) for m in range(owners - 1, 0, -1)
    ][::-1]
    descriptors = pl.pallas_call(
        lambda *refs: merge_kernel(owners, *refs),
        out_shape=jax.ShapeDtypeStruct((SLOTS, LANES), F32),
        in_specs=[vmem] * (owners + 1) + [smem],
        out_specs=vmem,
        compiler_params=params,
    )(*received, recv_slot.reshape(owners, offered), recv_count.reshape(1, owners))
    return (dog, descriptors.reshape(1, 1, SLOTS, LANES))


def solution(mesh):
    in_specs = (
        P("view", "bulk", None),
        P("bulk", "view", None, None),
        P("bulk", "view", None, None),
        P("bulk", "view", None),
    )
    out_specs = (P(None, "bulk", "view"), P("bulk", "view", None, None))
    return jax.shard_map(local, mesh=mesh, in_specs=in_specs, out_specs=out_specs, check_vma=False)
```

time: 117 us -> 39 us (0.33)
  other arithmetic: 44.6 us -> 0 us
  waiting for transfers between devices: 29.2 us -> 11.3 us
  local copies, waits for them, and re-layouts: 18.7 us -> 1.7 us
  Pallas kernels: 0 us -> 7.39 us
  starting transfers between devices: 20.9 us -> 17.6 us
  matrix products: 1.44 us -> 0 us
    add x6 -> x0, other arithmetic: 35.7 us -> none  [the longest x3 35.6 us: smooth(): total = term if total is None else total + term]
    all_to_all x2 -> x0, waiting for transfers between devices: 20.3 us -> none  [the longest x1 14.4 us: local(): lax.all_to_all(main, 'view', split_axis=2, concat_axis=0, tiled=True)]
    all_to_all x2 -> x0, starting transfers between devices: 15.7 us -> none  [the longest x1 9.4 us: local(): lax.all_to_all(chosen, 'bulk', split_axis=0, concat_axis=0, tiled=True)]
    ppermute x4 -> x15, starting transfers between devices: 5.2 us -> 17.6 us  [the longest x14 17 us: swap(): return lax.ppermute(block, axis, [(i, i ^ distance) for i in range(count)])]
    pallas_call x0 -> x4, Pallas kernels: none -> 7.39 us  [the longest x1 4.98 us: local(): pl.pallas_call(lambda *refs: filter_kernel(views, owners, *refs), out_sha...]
    slice x4 -> x0, local copies, waits for them, and re-layouts: 7.1 us -> none  [the longest x3 4.93 us: with_halo(): lax.slice_in_dim(block, block.shape[dim] - width, None, axis=dim)]
    mul x1 -> x0, other arithmetic: 5.54 us -> none  [smooth(): term = weights[:, offset].reshape((2,) + (1,) * (fields.ndim - 1)) * shifted]
    ppermute x2 -> x0, local copies, waits for them, and re-layouts: 4.89 us -> none  [the longest x1 2.94 us: with_halo(): lax.ppermute(lax.slice_in_dim(block, 0, width, axis=dim), axis, backward)]
  transfers between devices with their start and end apart: 6 -> 15, of which waited for: 5 -> 5; matrix products, arithmetic and copies ran while one was open for 4% -> 0% of each run, Pallas kernels for 0% -> 0%
where the time goes in v1:
time: 39 us; the launch traced here: 38.8 us
  starting transfers between devices  17.6 us (45%)
  waiting for transfers between devices  11.3 us (29%)
  Pallas kernels  7.39 us (19%)
  local copies, waits for them, and re-layouts  1.7 us (4%)
  between operations  0.73 us (2%)
    ppermute x14, starting transfers between devices, swap(): return lax.ppermute(block, axis, [(i, i ^ distance) for i in range(count)])  17 us
    ppermute x14, waiting for transfers between devices, swap(): return lax.ppermute(block, axis, [(i, i ^ distance) for i in range(count)])  11.3 us
    pallas_call x1, Pallas kernels, local(): pl.pallas_call(lambda *refs: filter_kernel(views, owners, *refs), out_sha...  4.98 us
    pallas_call x1, Pallas kernels, local(): pl.pallas_call(lambda *refs: merge_kernel(owners, *refs), out_shape=jax.S...  2.11 us
    unnamed x12, local copies, waits for them, and re-layouts  1.7 us
  transfers between devices with their start and end apart: 15, of which 5 were waited for; matrix products, arithmetic and copies ran while one was open for 0% of the time, Pallas kernels for 0%

profile of v1, /device:TPU:0, one launch (start us, length us, event | category | flops | bytes accessed | tf_op | source)
XLA Modules:
  0.0 38.8 jit_solution(4855862350635354706)
XLA Ops:
  0.6 0.0 copy-start
  0.6 1.0 %copy-done = bf16[8,64,512]{2,1,0:T(8,128)(2,1)S(1)} copy-done((bf16[8,64,512]{2,1,0:T(8,128)(2,1)S(1)}, bf16[8,64,512]{2,1,0:T(8,128)(2,1)}, u32[]{:S(2)}) %copy-start) | copy-done | bytes 524312
  1.7 0.0 copy-start.1
  1.7 0.3 shard_map.77
  2.0 0.0 copy-start.2
  2.0 3.1 %collective-permute-start = (bf16[2,80,128]{2,1,0:T(8,128)(2,1)S(1)}, bf16[2,80,128]{2,1,0:T(8,128)(2,1)S(1)}, u32[]{:S(2)}, u32[]{:S(2)}) collective-permute-start(bf16[2,80,128]{2,1,0:T(8,128)(2,1)S(1)} %get-tuple-element.22), channel_id=1, source_target_pairs={{0,1},{1,0},{2,3},{3,2},{4,5},{5,4},{6,7},{7,6},{8,9},{9,8},{10,11... | collective-permute-start | bytes 122888 | tf_op jit(solution)/shard_map/ppermute | solution.py:251
  5.1 2.6 %collective-permute-start.1 = (bf16[2,80,128]{2,1,0:T(8,128)(2,1)S(1)}, bf16[2,80,128]{2,1,0:T(8,128)(2,1)S(1)}, u32[]{:S(2)}, u32[]{:S(2)}) collective-permute-start(bf16[2,80,128]{2,1,0:T(8,128)(2,1)S(1)} %get-tuple-element.23), channel_id=1, source_target_pairs={{0,2},{1,3},{2,0},{3,1},{4,6},{5,7},{6,4},{7,5},{8,10},{9,11},{10,... | collective-permute-start | bytes 122888 | tf_op jit(solution)/shard_map/ppermute | solution.py:251
  7.6 0.0 collective-permute-start.2
  7.6 0.9 %collective-permute-start.3 = (bf16[9,48,128]{2,1,0:T(8,128)(2,1)S(1)}, bf16[9,48,128]{2,1,0:T(8,128)(2,1)S(1)}, u32[]{:S(2)}, u32[]{:S(2)}) collective-permute-start(bf16[9,48,128]{2,1,0:T(8,128)(2,1)S(1)} %get-tuple-element.26), channel_id=1, source_target_pairs={{0,1},{1,0},{2,3},{3,2},{4,5},{5,4},{6,7},{7,6},{8,9},{9,8},{10,11... | collective-permute-start | bytes 331784 | tf_op jit(solution)/shard_map/ppermute | solution.py:251
  8.5 3.5 %collective-permute-start.4 = (bf16[9,48,128]{2,1,0:T(8,128)(2,1)S(1)}, bf16[9,48,128]{2,1,0:T(8,128)(2,1)S(1)}, u32[]{:S(2)}, u32[]{:S(2)}) collective-permute-start(bf16[9,48,128]{2,1,0:T(8,128)(2,1)S(1)} %get-tuple-element.27), channel_id=1, source_target_pairs={{0,2},{1,3},{2,0},{3,1},{4,6},{5,7},{6,4},{7,5},{8,10},{9,11},{10,... | collective-permute-start | bytes 331784 | tf_op jit(solution)/shard_map/ppermute | solution.py:251
  12.0 0.0 collective-permute-done.refs_1_
  12.0 0.0 collective-permute-start.5
  12.0 0.0 collective-permute-done.1.refs_2_
  12.0 2.0 %collective-permute-done.2.refs_3_ = bf16[2,80,128]{2,1,0:T(8,128)(2,1)S(1)} collective-permute-done((bf16[2,80,128]{2,1,0:T(8,128)(2,1)S(1)}, bf16[2,80,128]{2,1,0:T(8,128)(2,1)S(1)}, u32[]{:S(2)}, u32[]{:S(2)}) %collective-permute-start.2) | collective-permute-done | bytes 40992 | tf_op jit(solution)/shard_map/ppermute | solution.py:251
  14.1 0.0 copy-start.3
  14.1 0.1 collective-permute-start.6
  14.2 0.7 %collective-permute-start.7 = (bf16[4,80,128]{2,1,0:T(8,128)(2,1)S(1)}, bf16[4,80,128]{2,1,0:T(8,128)(2,1)S(1)}, u32[]{:S(2)}, u32[]{:S(2)}) collective-permute-start(bf16[4,80,128]{2,1,0:T(8,128)(2,1)S(1)} %get-tuple-element.30), channel_id=1, source_target_pairs={{4,8},{12,16},{20,24},{8,4},{16,12},{24,20},{5,9},{13,17},{21,25},... | collective-permute-start | bytes 245768 | tf_op jit(solution)/shard_map/ppermute | solution.py:288
  14.8 0.0 collective-permute-done.3.refs_5_
  14.8 5.8 %collective-permute-done.4.refs_6_ = bf16[9,48,128]{2,1,0:T(8,128)(2,1)S(1)} collective-permute-done((bf16[9,48,128]{2,1,0:T(8,128)(2,1)S(1)}, bf16[9,48,128]{2,1,0:T(8,128)(2,1)S(1)}, u32[]{:S(2)}, u32[]{:S(2)}) %collective-permute-start.4) | collective-permute-done | bytes 110624 | tf_op jit(solution)/shard_map/ppermute | solution.py:251
  20.6 0.0 collective-permute-done.5.refs_7_
  20.7 0.0 collective-permute-done.6.refs_8_
  20.7 0.0 collective-permute-done.7.refs_9_
  20.7 0.0 copy-done.1
  20.7 0.0 copy-done.2
  20.7 0.0 copy-done.3
  20.7 5.0 %shard_map.79 = (bf16[32,64,128]{2,1,0:T(8,128)(2,1)}, bf16[128,128]{1,0:T(8,128)(2,1)S(1)}, bf16[128,128]{1,0:T(8,128)(2,1)S(1)}, bf16[128,128]{1,0:T(8,128)(2,...) custom-call(bf16[2,80,128]{2,1,0:T(8,128)(2,1)S(1)} %get-tuple-eleme, ...), custom_call_target="tpu_custom_call" | custom-call | tf_op jit(solution)/shard_map/pallas_call | solution.py:290
  25.7 0.4 collective-permute-start.8
  26.1 2.1 %collective-permute-start.9 = (bf16[128,128]{1,0:T(8,128)(2,1)S(1)}, bf16[128,128]{1,0:T(8,128)(2,1)S(1)}, u32[]{:S(2)}, u32[]{:S(2)}) collective-permute-start(bf16[128,128]{1,0:T(8,128)(2,1)S(1)} %get-tuple-element.34), channel_id=1, source_target_pairs={{0,8},{4,12},{8,0},{12,4},{16,24},{20,28},{24,16},{28,20},{1,9},{5... | collective-permute-start | bytes 98312 | tf_op jit(solution)/shard_map/ppermute | solution.py:251
  28.1 0.0 collective-permute-start.10
  28.1 1.7 %collective-permute-start.11 = (bf16[128,128]{1,0:T(8,128)(2,1)S(1)}, bf16[128,128]{1,0:T(8,128)(2,1)S(1)}, u32[]{:S(2)}, u32[]{:S(2)}) collective-permute-start(bf16[128,128]{1,0:T(8,128)(2,1)S(1)} %get-tuple-element.36), channel_id=1, source_target_pairs={{0,16},{4,20},{8,24},{12,28},{16,0},{20,4},{24,8},{28,12},{1,17},{... | collective-permute-start | bytes 98312 | tf_op jit(solution)/shard_map/ppermute | solution.py:251
  29.9 0.0 collective-permute-start.12
  29.9 0.0 collective-permute-done.8.refs_1_
  29.9 0.0 copy-start.4
  29.9 1.9 %collective-permute-start.13 = (bf16[128,128]{1,0:T(8,128)(2,1)S(1)}, bf16[128,128]{1,0:T(8,128)(2,1)S(1)}, u32[]{:S(2)}, u32[]{:S(2)}) collective-permute-start(bf16[128,128]{1,0:T(8,128)(2,1)S(1)} %get-tuple-element.38), channel_id=1, source_target_pairs={{0,24},{4,28},{8,16},{12,20},{16,8},{20,12},{24,0},{28,4},{1,25},{... | collective-permute-start | bytes 98312 | tf_op jit(solution)/shard_map/ppermute | solution.py:251
  31.8 0.0 collective-permute-done.9.refs_2_
  31.8 0.8 %collective-permute-start.14 = (bf16[128,128]{1,0:T(8,128)(2,1)S(1)}, bf16[128,128]{1,0:T(8,128)(2,1)S(1)}, u32[]{:S(2)}, u32[]{:S(2)}) collective-permute-start(bf16[128,128]{1,0:T(8,128)(2,1)S(1)} %get-tuple-element.39), channel_id=1, source_target_pairs={{0,28},{4,24},{8,20},{12,16},{16,12},{20,8},{24,4},{28,0},{1,29},{... | collective-permute-start | bytes 98312 | tf_op jit(solution)/shard_map/ppermute | solution.py:251
  32.5 0.0 collective-permute-done.10.refs_3_
  32.5 0.0 collective-permute-done.11.refs_4_
  32.5 0.8 %collective-permute-done.12.refs_5_ = bf16[128,128]{1,0:T(8,128)(2,1)S(1)} collective-permute-done((bf16[128,128]{1,0:T(8,128)(2,1)S(1)}, bf16[128,128]{1,0:T(8,128)(2,1)S(1)}, u32[]{:S(2)}, u32[]{:S(2)}) %collective-permute-start.12) | collective-permute-done | bytes 32800 | tf_op jit(solution)/shard_map/ppermute | solution.py:251
  33.3 1.4 %collective-permute-done.13.refs_6_ = bf16[128,128]{1,0:T(8,128)(2,1)S(1)} collective-permute-done((bf16[128,128]{1,0:T(8,128)(2,1)S(1)}, bf16[128,128]{1,0:T(8,128)(2,1)S(1)}, u32[]{:S(2)}, u32[]{:S(2)}) %collective-permute-start.13) | collective-permute-done | bytes 32800 | tf_op jit(solution)/shard_map/ppermute | solution.py:251
  34.8 1.2 %collective-permute-done.14.refs_7_ = bf16[128,128]{1,0:T(8,128)(2,1)S(1)} collective-permute-done((bf16[128,128]{1,0:T(8,128)(2,1)S(1)}, bf16[128,128]{1,0:T(8,128)(2,1)S(1)}, u32[]{:S(2)}, u32[]{:S(2)}) %collective-permute-start.14) | collective-permute-done | bytes 32800 | tf_op jit(solution)/shard_map/ppermute | solution.py:251
  36.0 0.0 copy-start.5
  36.0 0.0 copy-done.4
  36.0 0.7 %copy-done.5 = s32[1,1,8]{2,1,0:T(1,128)S(1)} copy-done((s32[1,1,8]{2,1,0:T(1,128)S(1)}, s32[1,1,8]{2,1,0:T(1,128)}, u32[]{:S(2)}) %copy-start.5) | copy-done | bytes 56
  36.7 2.1 %shard_map.80 = f32[1024,128]{1,0:T(8,128)} custom-call(bf16[128,128]{1,0:T(8,128)(2,1)S(1)} %get-tuple-element.32.refs_0_, bf16[128,128]{1,0:T(8,128)(2,1)S(1)} %collective-permute-done.8.refs_1_, bf16[128,128]{1,0:T(8,128)(2,1)S(1)} %collective-permute-done.9.refs_2_, bf16[128,128]{1,0:T(8,128)(2,1)S(1)} %collective-permute-done.10.refs_3_, ...), custom_call_target="tpu_custom_call" | custom-call | tf_op jit(solution)/shard_map/pallas_call | solution.py:310
  (1 shorter events, 0.0 us)
Async XLA Ops:
  0.6 1.0 %copy-start = (bf16[8,64,512]{2,1,0:T(8,128)(2,1)S(1)}, bf16[8,64,512]{2,1,0:T(8,128)(2,1)}, u32[]{:S(2)}) copy-start(bf16[8,64,512]{2,1,0:T(8,128)(2,1)} %planes_ref.1) | copy-start | bytes 1572868
  1.7 19.0 %copy-start.1 = (bf16[2,256,256]{2,1,0:T(8,128)(2,1)S(1)}, bf16[2,256,256]{2,1,0:T(8,128)(2,1)}, u32[]{:S(2)}) copy-start(bf16[2,256,256]{2,1,0:T(8,128)(2,1)} %constant.4.clone.refs_10_) | copy-start | bytes 786436
  2.0 18.7 %copy-start.2 = (bf16[2,2,64,256]{3,2,1,0:T(8,128)(2,1)S(1)}, bf16[2,2,64,256]{3,2,1,0:T(8,128)(2,1)}, u32[]{:S(2)}) copy-start(bf16[2,2,64,256]{3,2,1,0:T(8,128)(2,1)} %constant.5.clone.refs_11_) | copy-start | bytes 393220
  2.0 10.1 %collective-permute-start = (bf16[2,80,128]{2,1,0:T(8,128)(2,1)S(1)}, bf16[2,80,128]{2,1,0:T(8,128)(2,1)S(1)}, u32[]{:S(2)}, u32[]{:S(2)}) collective-permute-start(bf16[2,80,128]{2,1,0:T(8,128)(2,1)S(1)} %get-tuple-element.22), channel_id=1, source_target_pairs={{0,1},{1,0},{2,3},{3,2},{4,5},{5,4},{6,7},{7,6},{8,9},{9,8},{10,11... | collective-permute-start | bytes 122888 | tf_op jit(solution)/shard_map/ppermute | solution.py:251
  5.1 7.0 %collective-permute-start.1 = (bf16[2,80,128]{2,1,0:T(8,128)(2,1)S(1)}, bf16[2,80,128]{2,1,0:T(8,128)(2,1)S(1)}, u32[]{:S(2)}, u32[]{:S(2)}) collective-permute-start(bf16[2,80,128]{2,1,0:T(8,128)(2,1)S(1)} %get-tuple-element.23), channel_id=1, source_target_pairs={{0,2},{1,3},{2,0},{3,1},{4,6},{5,7},{6,4},{7,5},{8,10},{9,11},{10,... | collective-permute-start | bytes 122888 | tf_op jit(solution)/shard_map/ppermute | solution.py:251
  7.6 6.4 %collective-permute-start.2 = (bf16[2,80,128]{2,1,0:T(8,128)(2,1)S(1)}, bf16[2,80,128]{2,1,0:T(8,128)(2,1)S(1)}, u32[]{:S(2)}, u32[]{:S(2)}) collective-permute-start(bf16[2,80,128]{2,1,0:T(8,128)(2,1)S(1)} %get-tuple-element.24), channel_id=1, source_target_pairs={{0,3},{1,2},{2,1},{3,0},{4,7},{5,6},{6,5},{7,4},{8,11},{9,10},{10,... | collective-permute-start | bytes 122888 | tf_op jit(solution)/shard_map/ppermute | solution.py:251
  7.6 7.2 %collective-permute-start.3 = (bf16[9,48,128]{2,1,0:T(8,128)(2,1)S(1)}, bf16[9,48,128]{2,1,0:T(8,128)(2,1)S(1)}, u32[]{:S(2)}, u32[]{:S(2)}) collective-permute-start(bf16[9,48,128]{2,1,0:T(8,128)(2,1)S(1)} %get-tuple-element.26), channel_id=1, source_target_pairs={{0,1},{1,0},{2,3},{3,2},{4,5},{5,4},{6,7},{7,6},{8,9},{9,8},{10,11... | collective-permute-start | bytes 331784 | tf_op jit(solution)/shard_map/ppermute | solution.py:251
  8.5 12.1 %collective-permute-start.4 = (bf16[9,48,128]{2,1,0:T(8,128)(2,1)S(1)}, bf16[9,48,128]{2,1,0:T(8,128)(2,1)S(1)}, u32[]{:S(2)}, u32[]{:S(2)}) collective-permute-start(bf16[9,48,128]{2,1,0:T(8,128)(2,1)S(1)} %get-tuple-element.27), channel_id=1, source_target_pairs={{0,2},{1,3},{2,0},{3,1},{4,6},{5,7},{6,4},{7,5},{8,10},{9,11},{10,... | collective-permute-start | bytes 331784 | tf_op jit(solution)/shard_map/ppermute | solution.py:251
  12.0 8.6 %collective-permute-start.5 = (bf16[9,48,128]{2,1,0:T(8,128)(2,1)S(1)}, bf16[9,48,128]{2,1,0:T(8,128)(2,1)S(1)}, u32[]{:S(2)}, u32[]{:S(2)}) collective-permute-start(bf16[9,48,128]{2,1,0:T(8,128)(2,1)S(1)} %get-tuple-element.28), channel_id=1, source_target_pairs={{0,3},{1,2},{2,1},{3,0},{4,7},{5,6},{6,5},{7,4},{8,11},{9,10},{10,... | collective-permute-start | bytes 331784 | tf_op jit(solution)/shard_map/ppermute | solution.py:251
  14.1 6.6 %copy-start.3 = (s32[1,1,8,128]{3,2,1,0:T(8,128)S(1)}, s32[1,1,8,128]{3,2,1,0:T(8,128)}, u32[]{:S(2)}) copy-start(s32[1,1,8,128]{3,2,1,0:T(8,128)} %param.7) | copy-start | bytes 12292
  14.1 6.6 %collective-permute-start.6 = (bf16[4,80,128]{2,1,0:T(8,128)(2,1)S(1)}, bf16[4,80,128]{2,1,0:T(8,128)(2,1)S(1)}, u32[]{:S(2)}, u32[]{:S(2)}) collective-permute-start(bf16[4,80,128]{2,1,0:T(8,128)(2,1)S(1)} %get-tuple-element.29), channel_id=1, source_target_pairs={{0,4},{4,0},{8,12},{12,8},{16,20},{20,16},{24,28},{28,24},{1,5},{5... | collective-permute-start | bytes 245768 | tf_op jit(solution)/shard_map/ppermute | solution.py:251
  14.2 6.5 %collective-permute-start.7 = (bf16[4,80,128]{2,1,0:T(8,128)(2,1)S(1)}, bf16[4,80,128]{2,1,0:T(8,128)(2,1)S(1)}, u32[]{:S(2)}, u32[]{:S(2)}) collective-permute-start(bf16[4,80,128]{2,1,0:T(8,128)(2,1)S(1)} %get-tuple-element.30), channel_id=1, source_target_pairs={{4,8},{12,16},{20,24},{8,4},{16,12},{24,20},{5,9},{13,17},{21,25},... | collective-permute-start | bytes 245768 | tf_op jit(solution)/shard_map/ppermute | solution.py:288
  25.7 4.2 %collective-permute-start.8 = (bf16[128,128]{1,0:T(8,128)(2,1)S(1)}, bf16[128,128]{1,0:T(8,128)(2,1)S(1)}, u32[]{:S(2)}, u32[]{:S(2)}) collective-permute-start(bf16[128,128]{1,0:T(8,128)(2,1)S(1)} %get-tuple-element.33), channel_id=1, source_target_pairs={{0,4},{4,0},{8,12},{12,8},{16,20},{20,16},{24,28},{28,24},{1,5},{5... | collective-permute-start | bytes 98312 | tf_op jit(solution)/shard_map/ppermute | solution.py:251
  26.1 5.7 %collective-permute-start.9 = (bf16[128,128]{1,0:T(8,128)(2,1)S(1)}, bf16[128,128]{1,0:T(8,128)(2,1)S(1)}, u32[]{:S(2)}, u32[]{:S(2)}) collective-permute-start(bf16[128,128]{1,0:T(8,128)(2,1)S(1)} %get-tuple-element.34), channel_id=1, source_target_pairs={{0,8},{4,12},{8,0},{12,4},{16,24},{20,28},{24,16},{28,20},{1,9},{5... | collective-permute-start | bytes 98312 | tf_op jit(solution)/shard_map/ppermute | solution.py:251
  28.1 4.4 %collective-permute-start.10 = (bf16[128,128]{1,0:T(8,128)(2,1)S(1)}, bf16[128,128]{1,0:T(8,128)(2,1)S(1)}, u32[]{:S(2)}, u32[]{:S(2)}) collective-permute-start(bf16[128,128]{1,0:T(8,128)(2,1)S(1)} %get-tuple-element.35), channel_id=1, source_target_pairs={{0,12},{4,8},{8,4},{12,0},{16,28},{20,24},{24,20},{28,16},{1,13},{... | collective-permute-start | bytes 98312 | tf_op jit(solution)/shard_map/ppermute | solution.py:251
  28.1 4.4 %collective-permute-start.11 = (bf16[128,128]{1,0:T(8,128)(2,1)S(1)}, bf16[128,128]{1,0:T(8,128)(2,1)S(1)}, u32[]{:S(2)}, u32[]{:S(2)}) collective-permute-start(bf16[128,128]{1,0:T(8,128)(2,1)S(1)} %get-tuple-element.36), channel_id=1, source_target_pairs={{0,16},{4,20},{8,24},{12,28},{16,0},{20,4},{24,8},{28,12},{1,17},{... | collective-permute-start | bytes 98312 | tf_op jit(solution)/shard_map/ppermute | solution.py:251
  29.9 3.5 %collective-permute-start.12 = (bf16[128,128]{1,0:T(8,128)(2,1)S(1)}, bf16[128,128]{1,0:T(8,128)(2,1)S(1)}, u32[]{:S(2)}, u32[]{:S(2)}) collective-permute-start(bf16[128,128]{1,0:T(8,128)(2,1)S(1)} %get-tuple-element.37), channel_id=1, source_target_pairs={{0,20},{4,16},{8,28},{12,24},{16,4},{20,0},{24,12},{28,8},{1,21},{... | collective-permute-start | bytes 98312 | tf_op jit(solution)/shard_map/ppermute | solution.py:251
  29.9 6.1 %copy-start.4 = (s32[1,1,8,128]{3,2,1,0:T(8,128)S(1)}, s32[1,1,8,128]{3,2,1,0:T(8,128)}, u32[]{:S(2)}) copy-start(s32[1,1,8,128]{3,2,1,0:T(8,128)} %param.8) | copy-start | bytes 12292
  29.9 4.9 %collective-permute-start.13 = (bf16[128,128]{1,0:T(8,128)(2,1)S(1)}, bf16[128,128]{1,0:T(8,128)(2,1)S(1)}, u32[]{:S(2)}, u32[]{:S(2)}) collective-permute-start(bf16[128,128]{1,0:T(8,128)(2,1)S(1)} %get-tuple-element.38), channel_id=1, source_target_pairs={{0,24},{4,28},{8,16},{12,20},{16,8},{20,12},{24,0},{28,4},{1,25},{... | collective-permute-start | bytes 98312 | tf_op jit(solution)/shard_map/ppermute | solution.py:251
  31.8 4.2 %collective-permute-start.14 = (bf16[128,128]{1,0:T(8,128)(2,1)S(1)}, bf16[128,128]{1,0:T(8,128)(2,1)S(1)}, u32[]{:S(2)}, u32[]{:S(2)}) collective-permute-start(bf16[128,128]{1,0:T(8,128)(2,1)S(1)} %get-tuple-element.39), channel_id=1, source_target_pairs={{0,28},{4,24},{8,20},{12,16},{16,12},{20,8},{24,4},{28,0},{1,29},{... | collective-permute-start | bytes 98312 | tf_op jit(solution)/shard_map/ppermute | solution.py:251
  36.0 0.7 %copy-start.5 = (s32[1,1,8]{2,1,0:T(1,128)S(1)}, s32[1,1,8]{2,1,0:T(1,128)}, u32[]{:S(2)}) copy-start(s32[1,1,8]{2,1,0:T(1,128)} %param.9) | copy-start | bytes 100

commit v2 on v0

v2 whole, which is shorter than its diff:
```python
import math

import jax
import jax.numpy as jnp
import numpy as np
from jax import lax
from jax.experimental import pallas as pl
from jax.experimental.pallas import tpu as pltpu
from jax.sharding import PartitionSpec as P

RADIUS = 8
SLOTS = 1024
LANES = 128
BLOCK = 256
TILE = 16

narrow_sigma = (1.0, 2.0, 2.0)
broad_sigma = (1.6, 3.2, 3.2)
contrast = 20.0
epsilon = 1e-06

F32 = jnp.float32
BF16 = jnp.bfloat16


def gauss_taps(sigma, radius):
    weights = [math.exp(-0.5 * (offset / sigma) ** 2) for offset in range(-radius, radius + 1)]
    scale_total = sum(weights)
    return [weight / scale_total for weight in weights]


def taps(along):
    return [
        np.asarray(gauss_taps(sigma[along], RADIUS), np.float32)
        for sigma in (narrow_sigma, broad_sigma)
    ]


def split_bf16(array):
    high = array.astype(jnp.bfloat16)
    low = (array - high.astype(np.float32)).astype(jnp.bfloat16)
    return high, low


def band(where_in, where_out, tap):
    offset = np.asarray(where_in)[:, None] - np.asarray(where_out)[None, :] + RADIUS
    inside = (offset >= 0) & (offset <= 2 * RADIUS)
    return np.where(inside, tap[np.clip(offset, 0, 2 * RADIUS)], 0).astype(np.float32)


def x_weights():
    outs = np.arange(LANES)
    margin = list(range(-RADIUS, 0)) + list(range(LANES, LANES + RADIUS))
    main = np.concatenate([band(outs, outs, tap) for tap in taps(2)], axis=1)
    edge = np.concatenate([band(margin, outs, tap) for tap in taps(2)], axis=1)
    edge = np.tile(edge, (LANES // (2 * RADIUS), 1))
    return (
        np.concatenate(split_bf16(main), axis=0),
        np.concatenate(split_bf16(edge), axis=0),
    )


def y_weights(rows):
    low_edge, high_edge = list(range(RADIUS)), list(range(rows - RADIUS, rows))
    interior = list(range(RADIUS, rows - RADIUS))
    return np.stack(
        [
            np.stack(
                [
                    np.concatenate(
                        split_bf16(band(edges + interior, np.arange(rows), tap).T) * 2, axis=1
                    )
                    for tap in taps(1)
                ]
            )
            for edges in (high_edge + low_edge, low_edge + high_edge)
        ]
    )


def y_margin_weights(rows, pairs):
    low_halo, high_halo = list(range(-RADIUS, 0)), list(range(rows, rows + RADIUS))
    outs = list(range(RADIUS)) + list(range(rows - RADIUS, rows))
    result = []
    for order in (high_halo + low_halo, low_halo + high_halo):
        wide = [
            np.concatenate(split_bf16(band(order, outs, tap).T) * 2, axis=1).astype(np.float32)
            for tap in taps(1)
        ]
        result.append(np.stack([np.kron(np.eye(pairs, dtype=np.float32), w) for w in wide]))
    return np.stack(result).astype(jnp.bfloat16)


def edge_rows(zlocal):
    return -(-(zlocal + 1) * RADIUS // 16) * 16


def column_tile(source, which):
    at = pl.ds(pl.multiple_of(which * LANES, LANES), LANES)
    return source(at)


def with_margin(source, dest, views, rows):
    lane = lax.broadcasted_iota(jnp.int32, (rows, LANES), 1)
    left = column_tile(source, jnp.maximum(dest - 1, 0))
    right = column_tile(source, jnp.minimum(dest + 1, views - 1))
    lowest = jnp.where(dest > 0, LANES - RADIUS, LANES)
    highest = jnp.where(dest < views - 1, RADIUS, 0)
    margin = jnp.where(lane < highest, right, jnp.where(lane >= lowest, left, 0.0))
    return column_tile(source, dest), margin


def place_margin(margin, z):
    return pltpu.roll(margin, (2 * RADIUS * z + RADIUS) % LANES, 1)


def pack_kernel(shifts, planes_ref, *outs):
    views = len(shifts)
    edges, inner = outs[:views], outs[views:]
    zlocal, rows = planes_ref.shape[:2]
    me = lax.axis_index("view")
    odd = lax.axis_index("bulk") % 2 == 1
    for k, shift in enumerate(shifts):
        groups = []
        packed = None
        for z in range(zlocal):
            main, margin = with_margin(
                lambda at: planes_ref[z, :, at].astype(F32), me ^ shift, views, rows
            )
            groups.append(main)
            placed = place_margin(margin, z)
            packed = placed if packed is None else packed + placed
        groups.append(packed)
        low = [g[:RADIUS] for g in groups]
        high = [g[rows - RADIUS :] for g in groups]
        pad = edges[k].shape[1] - len(groups) * RADIUS
        if pad:
            low.append(jnp.zeros((pad, LANES), F32))
            high.append(jnp.zeros((pad, LANES), F32))
        low, high = jnp.concatenate(low, axis=0), jnp.concatenate(high, axis=0)
        edges[k][0] = jnp.where(odd, low, high).astype(BF16)
        edges[k][1] = jnp.where(odd, high, low).astype(BF16)
        for g, group in enumerate(groups):
            inner[k][g] = group[RADIUS : rows - RADIUS].astype(BF16)


def margin_kernel(passed_ref, *refs):
    *edges, near_ref, far_ref, _ = refs
    del passed_ref
    for k, edge in enumerate(edges):
        near_ref[k] = edge[0]
        far_ref[k] = edge[1]


def prepare_kernel(chips, main_ref, side_ref, wy_ref, wr_ref, index_ref, slot_ref, count_ref, *outs):
    wm_ref, ws_ref, inside_ref, margin_ref, column_ref, target_ref = outs
    brick = lax.axis_index("bulk")
    wm_ref[...] = main_ref[...]
    inside_ref[...] = wy_ref[brick % 2]
    group = lax.broadcasted_iota(jnp.int32, side_ref.shape, 0) % LANES // (2 * RADIUS)
    for z in range(ws_ref.shape[0]):
        ws_ref[z] = jnp.where(group == z, side_ref[...].astype(F32), 0.0).astype(BF16)
    margin_ref[...] = wr_ref[brick % 2]
    wanted = jnp.concatenate(
        [index_ref[pl.ds(brick ^ c ^ core, 1), :] for c in chips for core in range(2)], axis=0
    )
    column_ref[...] = jnp.transpose(wanted.astype(F32))
    candidate = lax.broadcasted_iota(jnp.int32, slot_ref.shape, 1)
    target = jnp.where(candidate < count_ref[...], slot_ref[...], -1)
    target_ref[...] = target


def twice(block):
    return jnp.concatenate([block, block], axis=1)


def split_stack(data):
    high = data.astype(BF16)
    low = (data - high.astype(F32)).astype(BF16)
    return [high, high, low, low]


def z_pass(load, planes_z):
    data = [[load(f, z) for z in range(planes_z)] for f in range(2)]
    z_taps = taps(0)
    scale = (contrast, -contrast)
    out = []
    for z in range(planes_z):
        total = None
        for f in range(2):
            for reach in range(RADIUS + 1):
                weight = float(scale[f] * z_taps[f][RADIUS + reach])
                near = [z] if reach == 0 else [z - reach, z + reach]
                sides = [data[f][q] for q in near if 0 <= q < planes_z]
                if not sides:
                    continue
                both = sides[0] if len(sides) == 1 else sides[0] + sides[1]
                term = weight * both
                total = term if total is None else total + term
        out.append(total)
    return out


def inner_kernel(shifts, *refs):
    views = len(shifts)
    edges, inner = refs[:views], refs[views : 2 * views]
    wm_ref, ws_ref, wy_ref, dog_ref, edge_ref, *fields = refs[2 * views :]
    zlocal, rows = inner[0].shape[0] - 1, wy_ref.shape[1]
    planes_z = zlocal * views
    me = lax.axis_index("view")

    small = [[edges[k][part].astype(F32) for part in range(2)] for k in range(views)]

    def rows_of(k, g):
        top = [s[g * RADIUS : (g + 1) * RADIUS] for s in small[k]]
        return [jnp.concatenate(top, axis=0).astype(BF16), inner[k][g]]

    def stacked(z):
        return twice(jnp.concatenate([p for k in range(views) for p in rows_of(k, z)], axis=0))

    margins = stacked(zlocal)

    def x_pass(z):
        main = jnp.dot(stacked(z), wm_ref[...], preferred_element_type=F32)
        return main + jnp.dot(margins, ws_ref[z], preferred_element_type=F32)

    for z in range(0, zlocal, 2):
        pair = [x_pass(z), x_pass(z + 1)]
        for k in range(views):
            at = (me ^ shifts[k]) * zlocal + z
            for f in range(2):
                data = jnp.concatenate(
                    [
                        p[k * rows : (k + 1) * rows, f * LANES : (f + 1) * LANES]
                        for p in pair
                    ],
                    axis=1,
                )
                operand = jnp.concatenate(split_stack(data), axis=0)
                out = jnp.dot(wy_ref[f], operand, preferred_element_type=F32)
                fields[f][at] = out[:, :LANES]
                fields[f][at + 1] = out[:, LANES:]

    def tile(step, carry):
        start = step * TILE + RADIUS
        at = pl.ds(pl.multiple_of(start, RADIUS), TILE)
        to = pl.ds(pl.multiple_of(step * TILE, TILE), TILE)
        done = z_pass(lambda f, z: fields[f][z, at, :], planes_z)
        for z in range(planes_z):
            dog_ref[z, to, :] = done[z]
        return carry

    lax.fori_loop(0, (rows - 2 * RADIUS) // TILE, tile, 0)
    for f in range(2):
        edge_ref[f, :, :RADIUS] = fields[f][:, :RADIUS]
        edge_ref[f, :, RADIUS:] = fields[f][:, rows - RADIUS :]


def outer_kernel(shifts, chips, *refs):
    views = len(shifts)
    halo, refs = refs[:2], refs[2:]
    inner_ref, edge_ref, wm_ref, ws_ref, wy_ref, column_ref, dog_hbm = refs[:7]
    chosen = refs[7 : 7 + len(chips)]
    fields, dog_ref, written = refs[7 + len(chips) :]
    planes_z, rows = dog_ref.shape[:2]
    zlocal = planes_z // views
    both = 2 * RADIUS
    me = lax.axis_index("view")
    brick = lax.axis_index("bulk")
    ends = (brick == 0) | (brick == lax.axis_size("bulk") - 1)

    def margin(part, k):
        data = halo[part][k].astype(F32)
        return jnp.where(ends, 0.0, data) if part == 1 else data

    small = [[margin(part, k) for part in range(2)] for k in range(views)]

    def rows_of(k, g):
        return [s[g * RADIUS : (g + 1) * RADIUS] for s in small[k]]

    main = [p for k in range(views) for z in range(zlocal) for p in rows_of(k, z)]
    side = [p for k in range(views) for p in rows_of(k, zlocal)]
    main = twice(jnp.concatenate(main, axis=0).astype(BF16))
    side = twice(jnp.concatenate(side, axis=0).astype(BF16))
    main = jnp.dot(main, wm_ref[...], preferred_element_type=F32)
    side = [jnp.dot(side, ws_ref[z], preferred_element_type=F32) for z in range(zlocal)]
    for k in range(views):
        smooth = [
            main[(k * zlocal + z) * both : (k * zlocal + z + 1) * both]
            + side[z][k * both : (k + 1) * both]
            for z in range(zlocal)
        ]
        at = (me ^ shifts[k]) * zlocal
        for f in range(2):
            parts = []
            for z in range(0, zlocal, 2):
                parts += split_stack(
                    jnp.concatenate(
                        [p[:, f * LANES : (f + 1) * LANES] for p in smooth[z : z + 2]], axis=1
                    )
                )
            operand = jnp.concatenate(parts, axis=0)
            out = jnp.dot(wy_ref[f], operand, preferred_element_type=F32)
            for z in range(zlocal):
                row, lane = z // 2 * both, z % 2 * LANES
                fields[f, at + z] = (
                    edge_ref[f, at + z] + out[row : row + both, lane : lane + LANES]
                )

    done = z_pass(lambda f, z: fields[f, z], planes_z)
    for z in range(planes_z):
        whole = [done[z][:RADIUS], inner_ref[z], done[z][RADIUS:]]
        dog_ref[z] = jnp.concatenate(whole, axis=0).astype(BF16)

    parts = written.shape[0]
    copies = []
    for part in range(parts):
        span = pl.ds(part * (planes_z // parts), planes_z // parts)
        copies.append(
            pltpu.make_async_copy(dog_ref.at[span], dog_hbm.at[span], written.at[part])
        )
        copies[-1].start()

    half = planes_z * rows // 2
    flat = dog_ref[...].reshape(2 * half, LANES)
    flat = jnp.concatenate([flat[:half], flat[half:]], axis=1)
    columns = column_ref[...]
    offered = columns.shape[0]
    lane = lax.broadcasted_iota(jnp.int32, (offered, BLOCK), 1).astype(F32).astype(BF16)
    for m in range(2 * len(chips)):
        column = columns[:, m : m + 1]
        later = column >= half
        column = jnp.where(later, column - half, column)
        upper = jnp.floor(column * (1.0 / BLOCK))
        lower = column - BLOCK * upper
        onehot = []
        for j in range(half // BLOCK):
            here = jnp.where(upper == j, lower, -1.0).astype(BF16)
            onehot.append(jnp.where(lane == here, 1.0, 0.0).astype(BF16))
        onehot = jnp.concatenate(onehot, axis=1)
        picked = jnp.dot(onehot, flat, preferred_element_type=F32)
        picked = jnp.where(later, picked[:, LANES:], picked[:, :LANES])
        chosen[m // 2][m % 2] = picked.astype(BF16)
    for copy in copies:
        copy.wait()


def forward_kernel(*refs):
    *rows, out_ref = refs
    for c, row in enumerate(rows):
        out_ref[c] = row[1]


def merge_kernel(chips, *refs):
    rows = refs[: len(chips)]
    passed_ref, target_ref, out_hbm, out_ref, written = refs[len(chips) :]
    owners, offered = target_ref.shape
    slots = out_ref.shape[0]
    owner = lax.axis_index("bulk")
    copies = []
    received = jnp.concatenate(
        [r[0] for r in rows] + [passed_ref[c] for c in range(len(chips))], axis=0
    )
    target = jnp.concatenate(
        [target_ref[pl.ds(owner ^ c ^ core, 1), :] for core in range(2) for c in chips], axis=1
    )
    upper, lower = target >> 8, (target & (BLOCK - 1)).astype(F32)
    place = lax.broadcasted_iota(jnp.int32, (BLOCK, owners * offered), 0).astype(F32).astype(BF16)
    for block in range(slots // BLOCK):
        wanted = jnp.where(upper == block, lower, -1.0).astype(BF16)
        onehot = jnp.where(place == wanted, 1.0, 0.0).astype(BF16)
        summed = jnp.dot(onehot, received, preferred_element_type=F32)
        scale = lax.rsqrt(jnp.mean(summed * summed, axis=-1, keepdims=True) + epsilon)
        span = pl.ds(block * BLOCK, BLOCK)
        out_ref[span] = summed * scale
        copies.append(
            pltpu.make_async_copy(out_ref.at[span], out_hbm.at[span], written.at[block])
        )
        copies[-1].start()
    for copy in copies:
        copy.wait()


def swap(block, axis, distance):
    if distance == 0:
        return block
    count = lax.axis_size(axis)
    return lax.ppermute(block, axis, [(i, i ^ distance) for i in range(count)])


def local(planes, cand_index, recv_slot, recv_count):
    views = lax.axis_size("view")
    bricks = lax.axis_size("bulk")
    zlocal, rows, width = planes.shape
    planes_z = zlocal * views
    owners, offered = cand_index.shape[2:]
    vmem = pl.BlockSpec(memory_space=pltpu.VMEM)
    hbm = pl.BlockSpec(memory_space=pltpu.HBM)
    params = pltpu.CompilerParams(vmem_limit_bytes=48 * 1024 * 1024)
    edge = jax.ShapeDtypeStruct((2, edge_rows(zlocal), LANES), BF16)
    body = jax.ShapeDtypeStruct((zlocal + 1, rows - 2 * RADIUS, LANES), BF16)
    halo = jax.ShapeDtypeStruct((views, edge_rows(zlocal), LANES), BF16)
    targets = jax.ShapeDtypeStruct((owners, offered), jnp.int32)
    shifts = list(range(views - 1, -1, -1))
    chips = list(range(owners - 2, -1, -2))

    packed = pl.pallas_call(
        lambda *refs: pack_kernel(shifts, *refs),
        out_shape=[edge] * views + [body] * views,
        in_specs=[vmem],
        out_specs=[vmem] * (2 * views),
        compiler_params=params,
    )(planes)
    edges = [swap(e, "view", k) for e, k in zip(packed[:views], shifts)]
    inner = [swap(e, "view", k) for e, k in zip(packed[views:], shifts)]

    weights = [*x_weights(), y_weights(rows), y_margin_weights(rows, zlocal // 2)]
    main_w, side_w, inside_w, margin_w, columns, target = pl.pallas_call(
        lambda *refs: prepare_kernel(chips, *refs),
        out_shape=[
            jax.ShapeDtypeStruct(weights[0].shape, BF16),
            jax.ShapeDtypeStruct((zlocal,) + weights[1].shape, BF16),
            jax.ShapeDtypeStruct(weights[2].shape[1:], BF16),
            jax.ShapeDtypeStruct(weights[3].shape[1:], BF16),
            jax.ShapeDtypeStruct((offered, owners), F32),
            targets,
        ],
        in_specs=[vmem] * 7,
        out_specs=[vmem] * 6,
        compiler_params=params,
    )(
        *[jnp.asarray(w) for w in weights],
        cand_index.reshape(owners, offered),
        recv_slot.reshape(owners, offered),
        recv_count.reshape(owners, 1),
    )
    near, far, target = pl.pallas_call(
        margin_kernel,
        out_shape=[halo] * 2 + [targets],
        in_specs=[vmem] * (views + 1),
        out_specs=[vmem] * 3,
        input_output_aliases={0: 2},
        compiler_params=params,
    )(target, *edges)
    far_pairs = [(i, i + 1) for i in range(1, bricks - 1, 2)] + [(0, bricks - 1)]
    far_pairs = far_pairs + [(target, source) for source, target in far_pairs]
    far = lax.ppermute(far, "bulk", far_pairs)
    near = swap(near, "bulk", 1)

    dog, sides = pl.pallas_call(
        lambda *refs: inner_kernel(shifts, *refs),
        out_shape=[
            jax.ShapeDtypeStruct((planes_z, rows - 2 * RADIUS, LANES), F32),
            jax.ShapeDtypeStruct((2, planes_z, 2 * RADIUS, LANES), F32),
        ],
        in_specs=[vmem] * (2 * views + 3),
        out_specs=[vmem] * 2,
        scratch_shapes=[pltpu.VMEM((planes_z, rows, LANES), F32)] * 2,
        compiler_params=params,
    )(*edges, *inner, main_w, side_w, inside_w)

    offers = jax.ShapeDtypeStruct((2, offered, LANES), BF16)
    dog, *chosen = pl.pallas_call(
        lambda *refs: outer_kernel(shifts, chips, *refs),
        out_shape=[jax.ShapeDtypeStruct((planes_z, rows, LANES), BF16)] + [offers] * len(chips),
        in_specs=[vmem] * 8,
        out_specs=[hbm] + [vmem] * len(chips),
        scratch_shapes=[
            pltpu.VMEM((2, planes_z, 2 * RADIUS, LANES), F32),
            pltpu.VMEM((planes_z, rows, LANES), BF16),
            pltpu.SemaphoreType.DMA((8,)),
        ],
        compiler_params=params,
    )(
        near,
        far,
        dog,
        sides,
        main_w,
        side_w,
        margin_w,
        columns,
    )
    received = [swap(c, "bulk", k) for c, k in zip(chosen, chips)]
    passed = pl.pallas_call(
        forward_kernel,
        out_shape=jax.ShapeDtypeStruct((len(chips), offered, LANES), BF16),
        in_specs=[vmem] * len(chips),
        out_specs=vmem,
        compiler_params=params,
    )(*received)
    passed = swap(passed, "bulk", 1)
    descriptors = pl.pallas_call(
        lambda *refs: merge_kernel(chips, *refs),
        out_shape=jax.ShapeDtypeStruct((SLOTS, LANES), F32),
        in_specs=[vmem] * (len(chips) + 2),
        out_specs=hbm,
        scratch_shapes=[
            pltpu.VMEM((SLOTS, LANES), F32),
            pltpu.SemaphoreType.DMA((SLOTS // BLOCK,)),
        ],
        compiler_params=params,
    )(*received, passed, target)
    return (dog, descriptors.reshape(1, 1, SLOTS, LANES))


def solution(mesh):
    in_specs = (
        P("view", "bulk", None),
        P("bulk", "view", None, None),
        P("bulk", "view", None, None),
        P("bulk", "view", None),
    )
    out_specs = (P(None, "bulk", "view"), P("bulk", "view", None, None))
    return jax.shard_map(local, mesh=mesh, in_specs=in_specs, out_specs=out_specs, check_vma=False)
```

time: 117 us -> 37.8 us (0.32)
  other arithmetic: 44.6 us -> 0 us
  waiting for transfers between devices: 29.2 us -> 10.4 us
  local copies, waits for them, and re-layouts: 18.7 us -> 1.75 us
  Pallas kernels: 0 us -> 8.3 us
  starting transfers between devices: 20.9 us -> 16.4 us
  matrix products: 1.44 us -> 0 us
    add x6 -> x0, other arithmetic: 35.7 us -> none  [the longest x3 35.6 us: smooth(): total = term if total is None else total + term]
    all_to_all x2 -> x0, waiting for transfers between devices: 20.3 us -> none  [the longest x1 14.4 us: local(): lax.all_to_all(main, 'view', split_axis=2, concat_axis=0, tiled=True)]
    all_to_all x2 -> x0, starting transfers between devices: 15.7 us -> none  [the longest x1 9.4 us: local(): lax.all_to_all(chosen, 'bulk', split_axis=0, concat_axis=0, tiled=True)]
    ppermute x4 -> x12, starting transfers between devices: 5.2 us -> 16.4 us  [the longest x11 13.8 us: swap(): return lax.ppermute(block, axis, [(i, i ^ distance) for i in range(count)])]
    pallas_call x0 -> x7, Pallas kernels: none -> 8.3 us  [the longest x1 3.11 us: local(): pl.pallas_call(lambda *refs: inner_kernel(shifts, *refs), out_shape=[jax....]
    slice x4 -> x0, local copies, waits for them, and re-layouts: 7.1 us -> none  [the longest x3 4.93 us: with_halo(): lax.slice_in_dim(block, block.shape[dim] - width, None, axis=dim)]
    mul x1 -> x0, other arithmetic: 5.54 us -> none  [smooth(): term = weights[:, offset].reshape((2,) + (1,) * (fields.ndim - 1)) * shifted]
    ppermute x2 -> x0, local copies, waits for them, and re-layouts: 4.89 us -> none  [the longest x1 2.94 us: with_halo(): lax.ppermute(lax.slice_in_dim(block, 0, width, axis=dim), axis, backward)]
  transfers between devices with their start and end apart: 6 -> 12, of which waited for: 5 -> 6; matrix products, arithmetic and copies ran while one was open for 4% -> 0% of each run, Pallas kernels for 0% -> 9%
where the time goes in v2:
time: 37.8 us; the launch traced here: 37.6 us
  starting transfers between devices  16.4 us (43%)
  waiting for transfers between devices  10.4 us (28%)
  Pallas kernels  8.3 us (22%)
  local copies, waits for them, and re-layouts  1.75 us (5%)
  between operations  0.72 us (2%)
    ppermute x11, starting transfers between devices, swap(): return lax.ppermute(block, axis, [(i, i ^ distance) for i in range(count)])  13.8 us
    ppermute x11, waiting for transfers between devices, swap(): return lax.ppermute(block, axis, [(i, i ^ distance) for i in range(count)])  10.4 us
    pallas_call x1, Pallas kernels, local(): pl.pallas_call(lambda *refs: inner_kernel(shifts, *refs), out_shape=[jax....  3.11 us
    pallas_call x1, Pallas kernels, local(): pl.pallas_call(lambda *refs: outer_kernel(shifts, chips, *refs), out_shap...  3.03 us
    ppermute x1, starting transfers between devices, local(): far = lax.ppermute(far, 'bulk', far_pairs)  2.55 us
    pallas_call x1, Pallas kernels, local(): pl.pallas_call(lambda *refs: merge_kernel(chips, *refs), out_shape=jax.Sh...  1.73 us
    unnamed x16, local copies, waits for them, and re-layouts  1.67 us
  transfers between devices with their start and end apart: 12, of which 6 were waited for; matrix products, arithmetic and copies ran while one was open for 0% of the time, Pallas kernels for 9%

profile of v2, /device:TPU:0, one launch (start us, length us, event | category | flops | bytes accessed | tf_op | source)
XLA Modules:
  0.0 37.6 jit_solution(15831330592658580113)
XLA Ops:
  0.6 0.0 copy-start
  0.6 1.0 %copy-done = bf16[8,64,512]{2,1,0:T(8,128)(2,1)S(1)} copy-done((bf16[8,64,512]{2,1,0:T(8,128)(2,1)S(1)}, bf16[8,64,512]{2,1,0:T(8,128)(2,1)}, u32[]{:S(2)}) %copy-start) | copy-done | bytes 524312
  1.7 0.0 copy-start.1
  1.7 0.0 copy-start.2
  1.7 0.0 copy-start.3
  1.7 0.0 copy-start.4
  1.7 0.3 shard_map.96
  2.0 5.1 %collective-permute-start = (bf16[2,80,128]{2,1,0:T(8,128)(2,1)S(1)}, bf16[2,80,128]{2,1,0:T(8,128)(2,1)S(1)}, u32[]{:S(2)}, u32[]{:S(2)}) collective-permute-start(bf16[2,80,128]{2,1,0:T(8,128)(2,1)S(1)} %get-tuple-element.27), channel_id=1, source_target_pairs={{0,3},{1,2},{2,1},{3,0},{4,7},{5,6},{6,5},{7,4},{8,11},{9,10},{10,... | collective-permute-start | bytes 122888 | tf_op jit(solution)/shard_map/ppermute | solution.py:388
  7.1 0.0 collective-permute-start.1
  7.1 0.6 %collective-permute-start.2 = (bf16[2,80,128]{2,1,0:T(8,128)(2,1)S(1)}, bf16[2,80,128]{2,1,0:T(8,128)(2,1)S(1)}, u32[]{:S(2)}, u32[]{:S(2)}) collective-permute-start(bf16[2,80,128]{2,1,0:T(8,128)(2,1)S(1)} %get-tuple-element.29), channel_id=1, source_target_pairs={{0,1},{1,0},{2,3},{3,2},{4,5},{5,4},{6,7},{7,6},{8,9},{9,8},{10,11... | collective-permute-start | bytes 122888 | tf_op jit(solution)/shard_map/ppermute | solution.py:388
  7.7 3.7 %collective-permute-start.5 = (bf16[9,48,128]{2,1,0:T(8,128)(2,1)S(1)}, bf16[9,48,128]{2,1,0:T(8,128)(2,1)S(1)}, u32[]{:S(2)}, u32[]{:S(2)}) collective-permute-start(bf16[9,48,128]{2,1,0:T(8,128)(2,1)S(1)} %get-tuple-element.33), channel_id=1, source_target_pairs={{0,3},{1,2},{2,1},{3,0},{4,7},{5,6},{6,5},{7,4},{8,11},{9,10},{10,... | collective-permute-start | bytes 331784 | tf_op jit(solution)/shard_map/ppermute | solution.py:388
  11.5 0.0 collective-permute-start.6
  11.5 0.0 collective-permute-done.refs_0_
  11.5 0.0 copy-start.7
  11.5 0.6 %collective-permute-start.7 = (bf16[9,48,128]{2,1,0:T(8,128)(2,1)S(1)}, bf16[9,48,128]{2,1,0:T(8,128)(2,1)S(1)}, u32[]{:S(2)}, u32[]{:S(2)}) collective-permute-start(bf16[9,48,128]{2,1,0:T(8,128)(2,1)S(1)} %get-tuple-element.35), channel_id=1, source_target_pairs={{0,1},{1,0},{2,3},{3,2},{4,5},{5,4},{6,7},{7,6},{8,9},{9,8},{10,11... | collective-permute-start | bytes 331784 | tf_op jit(solution)/shard_map/ppermute | solution.py:388
  12.1 0.0 copy-done.7
  12.1 0.0 copy-start.5
  12.1 0.0 copy-start.6
  12.1 0.1 copy.11.refs_6_
  12.2 0.0 copy-done.1
  12.2 0.0 copy-done.2
  12.2 0.0 copy-done.3
  12.2 0.0 copy-done.4
  12.2 0.6 %copy-done.5 = s32[1,1,8,128]{3,2,1,0:T(8,128)S(1)} copy-done((s32[1,1,8,128]{3,2,1,0:T(8,128)S(1)}, s32[1,1,8,128]{3,2,1,0:T(8,128)}, u32[]{:S(2)}) %copy-start.5) | copy-done | bytes 4120
  12.8 0.0 copy-done.6
  12.8 0.1 shard_map.95
  13.0 2.8 %collective-permute-done.1.refs_1_ = bf16[2,80,128]{2,1,0:T(8,128)(2,1)S(1)} collective-permute-done((bf16[2,80,128]{2,1,0:T(8,128)(2,1)S(1)}, bf16[2,80,128]{2,1,0:T(8,128)(2,1)S(1)}, u32[]{:S(2)}, u32[]{:S(2)}) %collective-permute-start.1) | collective-permute-done | bytes 40992 | tf_op jit(solution)/shard_map/ppermute | solution.py:388
  15.7 0.0 collective-permute-done.2.refs_2_
  15.8 0.1 collective-permute-start.3
  15.8 2.5 %collective-permute-start.4 = (bf16[4,80,128]{2,1,0:T(8,128)(2,1)S(1)}, bf16[4,80,128]{2,1,0:T(8,128)(2,1)S(1)}, u32[]{:S(2)}, u32[]{:S(2)}) collective-permute-start(bf16[4,80,128]{2,1,0:T(8,128)(2,1)S(1)} %get-tuple-element.32), channel_id=1, source_target_pairs={{4,8},{12,16},{20,24},{0,28},{8,4},{16,12},{24,20},{28,0},{5,9},{1... | collective-permute-start | bytes 245768 | tf_op jit(solution)/shard_map/ppermute | solution.py:447
  18.4 0.0 collective-permute-done.5.refs_4_
  18.4 2.5 %collective-permute-done.6.refs_5_ = bf16[9,48,128]{2,1,0:T(8,128)(2,1)S(1)} collective-permute-done((bf16[9,48,128]{2,1,0:T(8,128)(2,1)S(1)}, bf16[9,48,128]{2,1,0:T(8,128)(2,1)S(1)}, u32[]{:S(2)}, u32[]{:S(2)}) %collective-permute-start.6) | collective-permute-done | bytes 110624 | tf_op jit(solution)/shard_map/ppermute | solution.py:388
  20.9 0.0 collective-permute-done.7.refs_6_
  20.9 3.1 %shard_map.98 = (f32[32,48,128]{2,1,0:T(8,128)S(1)}, f32[2,32,16,128]{3,2,1,0:T(8,128)S(1)}) custom-call(bf16[2,80,128]{2,1,0:T(8,128)(2,1)S(1)} %collective-permute-done.refs_0_, bf16[2,80,128]{2,1,0:T(8,128)(2,1)S(1)} %collective-permute-done.1.refs_1_, bf16[2,80,128]{2,1,0:T(8,128)(2,1)S(1)} %collective-permute-done.2.refs_2_, ...), custom_call_target="tpu_custom_call" | custom-call | tf_op jit(solution)/shard_map/pallas_call | solution.py:450
  24.1 0.0 collective-permute-done.3.refs_0_
  24.1 0.0 collective-permute-done.4.refs_1_
  24.1 3.0 %shard_map.99 = (bf16[32,64,128]{2,1,0:T(8,128)(2,1)}, bf16[2,128,128]{2,1,0:T(8,128)(2,1)S(1)}, bf16[2,128,128]{2,1,0:T(8,128)(2,1)S(1)}, bf16[2,128,128]{2,1,0:T(8,128)(2,1)S(1)}, bf16[2,128,128]{2,1,0:T(8,128)(2,1)S(1)}) custom-call(bf16[4,80,128]{2,1,0:T(8,128)(2,1)S(1)} %collective-permute-done.3.refs_0_, ...), custom_call_target="tpu_custom_call" | custom-call | tf_op jit(solution)/shard_map/pallas_call | solution.py:463
  27.1 2.5 %collective-permute-start.8 = (bf16[2,128,128]{2,1,0:T(8,128)(2,1)S(1)}, bf16[2,128,128]{2,1,0:T(8,128)(2,1)S(1)}, u32[]{:S(2)}, u32[]{:S(2)}) collective-permute-start(bf16[2,128,128]{2,1,0:T(8,128)(2,1)S(1)} %get-tuple-element.45), channel_id=1, source_target_pairs={{0,24},{4,28},{8,16},{12,20},{16,8},{20,12},{24,0},{28,4},{1,25},{... | collective-permute-start | bytes 196616 | tf_op jit(solution)/shard_map/ppermute | solution.py:388
  29.6 0.5 %collective-permute-start.9 = (bf16[2,128,128]{2,1,0:T(8,128)(2,1)S(1)}, bf16[2,128,128]{2,1,0:T(8,128)(2,1)S(1)}, u32[]{:S(2)}, u32[]{:S(2)}) collective-permute-start(bf16[2,128,128]{2,1,0:T(8,128)(2,1)S(1)} %get-tuple-element.46), channel_id=1, source_target_pairs={{0,16},{4,20},{8,24},{12,28},{16,0},{20,4},{24,8},{28,12},{1,17},{... | collective-permute-start | bytes 196616 | tf_op jit(solution)/shard_map/ppermute | solution.py:388
  30.1 0.5 %collective-permute-start.10 = (bf16[2,128,128]{2,1,0:T(8,128)(2,1)S(1)}, bf16[2,128,128]{2,1,0:T(8,128)(2,1)S(1)}, u32[]{:S(2)}, u32[]{:S(2)}) collective-permute-start(bf16[2,128,128]{2,1,0:T(8,128)(2,1)S(1)} %get-tuple-element.47), channel_id=1, source_target_pairs={{0,8},{4,12},{8,0},{12,4},{16,24},{20,28},{24,16},{28,20},{1,9},{5... | collective-permute-start | bytes 196616 | tf_op jit(solution)/shard_map/ppermute | solution.py:388
  30.7 1.9 %collective-permute-done.8.refs_0_ = bf16[2,128,128]{2,1,0:T(8,128)(2,1)S(1)} collective-permute-done((bf16[2,128,128]{2,1,0:T(8,128)(2,1)S(1)}, bf16[2,128,128]{2,1,0:T(8,128)(2,1)S(1)}, u32[]{:S(2)}, u32[]{:S(2)}) %collective-permute-start.8) | collective-permute-done | bytes 65568 | tf_op jit(solution)/shard_map/ppermute | solution.py:388
  32.5 1.4 %collective-permute-done.9.refs_1_ = bf16[2,128,128]{2,1,0:T(8,128)(2,1)S(1)} collective-permute-done((bf16[2,128,128]{2,1,0:T(8,128)(2,1)S(1)}, bf16[2,128,128]{2,1,0:T(8,128)(2,1)S(1)}, u32[]{:S(2)}, u32[]{:S(2)}) %collective-permute-start.9) | collective-permute-done | bytes 65568 | tf_op jit(solution)/shard_map/ppermute | solution.py:388
  33.9 0.5 %collective-permute-done.10.refs_2_ = bf16[2,128,128]{2,1,0:T(8,128)(2,1)S(1)} collective-permute-done((bf16[2,128,128]{2,1,0:T(8,128)(2,1)S(1)}, bf16[2,128,128]{2,1,0:T(8,128)(2,1)S(1)}, u32[]{:S(2)}, u32[]{:S(2)}) %collective-permute-start.10) | collective-permute-done | bytes 65568 | tf_op jit(solution)/shard_map/ppermute | solution.py:388
  34.4 0.1 collective-permute-start.11
  34.5 1.3 %collective-permute-done.11.refs_4_ = bf16[4,128,128]{2,1,0:T(8,128)(2,1)S(1)} collective-permute-done((bf16[4,128,128]{2,1,0:T(8,128)(2,1)S(1)}, bf16[4,128,128]{2,1,0:T(8,128)(2,1)S(1)}, u32[]{:S(2)}, u32[]{:S(2)}) %collective-permute-start.11) | collective-permute-done | bytes 131104 | tf_op jit(solution)/shard_map/ppermute | solution.py:388
  35.8 1.7 %shard_map.101 = f32[1024,128]{1,0:T(8,128)} custom-call(bf16[2,128,128]{2,1,0:T(8,128)(2,1)S(1)} %collective-permute-done.8.refs_0_, bf16[2,128,128]{2,1,0:T(8,128)(2,1)S(1)} %collective-permute-done.9.refs_1_, bf16[2,128,128]{2,1,0:T(8,128)(2,1)S(1)} %collective-permute-done.10.refs_2_, bf16[2,128,128]{2,1,0:T(8,128)(2,1)S(1)} %get-tuple-element.48.refs_3_, ...), custom_call_target="tpu_custom_call" | custom-call | tf_op jit(solution)/shard_map/pallas_call | solution.py:493
  (2 shorter events, 0.0 us)
Async XLA Ops:
  0.6 1.0 %copy-start = (bf16[8,64,512]{2,1,0:T(8,128)(2,1)S(1)}, bf16[8,64,512]{2,1,0:T(8,128)(2,1)}, u32[]{:S(2)}) copy-start(bf16[8,64,512]{2,1,0:T(8,128)(2,1)} %refs_0_.2) | copy-start | bytes 1572868
  1.7 10.6 %copy-start.1 = (bf16[2,2,64,256]{3,2,1,0:T(8,128)(2,1)S(1)}, bf16[2,2,64,256]{3,2,1,0:T(8,128)(2,1)}, u32[]{:S(2)}) copy-start(bf16[2,2,64,256]{3,2,1,0:T(8,128)(2,1)} %constant.11.clone.refs_3_) | copy-start | bytes 393220
  1.7 10.6 %copy-start.2 = (bf16[2,2,64,256]{3,2,1,0:T(8,128)(2,1)S(1)}, bf16[2,2,64,256]{3,2,1,0:T(8,128)(2,1)}, u32[]{:S(2)}) copy-start(bf16[2,2,64,256]{3,2,1,0:T(8,128)(2,1)} %constant.10.clone.refs_2_) | copy-start | bytes 393220
  1.7 10.6 %copy-start.3 = (bf16[256,256]{1,0:T(8,128)(2,1)S(1)}, bf16[256,256]{1,0:T(8,128)(2,1)}, u32[]{:S(2)}) copy-start(bf16[256,256]{1,0:T(8,128)(2,1)} %constant.9.clone.refs_1_) | copy-start | bytes 393220
  1.7 10.6 %copy-start.4 = (bf16[256,256]{1,0:T(8,128)(2,1)S(1)}, bf16[256,256]{1,0:T(8,128)(2,1)}, u32[]{:S(2)}) copy-start(bf16[256,256]{1,0:T(8,128)(2,1)} %constant.8.clone.refs_0_) | copy-start | bytes 393220
  2.0 9.5 %collective-permute-start = (bf16[2,80,128]{2,1,0:T(8,128)(2,1)S(1)}, bf16[2,80,128]{2,1,0:T(8,128)(2,1)S(1)}, u32[]{:S(2)}, u32[]{:S(2)}) collective-permute-start(bf16[2,80,128]{2,1,0:T(8,128)(2,1)S(1)} %get-tuple-element.27), channel_id=1, source_target_pairs={{0,3},{1,2},{2,1},{3,0},{4,7},{5,6},{6,5},{7,4},{8,11},{9,10},{10,... | collective-permute-start | bytes 122888 | tf_op jit(solution)/shard_map/ppermute | solution.py:388
  7.1 8.6 %collective-permute-start.1 = (bf16[2,80,128]{2,1,0:T(8,128)(2,1)S(1)}, bf16[2,80,128]{2,1,0:T(8,128)(2,1)S(1)}, u32[]{:S(2)}, u32[]{:S(2)}) collective-permute-start(bf16[2,80,128]{2,1,0:T(8,128)(2,1)S(1)} %get-tuple-element.28), channel_id=1, source_target_pairs={{0,2},{1,3},{2,0},{3,1},{4,6},{5,7},{6,4},{7,5},{8,10},{9,11},{10,... | collective-permute-start | bytes 122888 | tf_op jit(solution)/shard_map/ppermute | solution.py:388
  7.1 8.6 %collective-permute-start.2 = (bf16[2,80,128]{2,1,0:T(8,128)(2,1)S(1)}, bf16[2,80,128]{2,1,0:T(8,128)(2,1)S(1)}, u32[]{:S(2)}, u32[]{:S(2)}) collective-permute-start(bf16[2,80,128]{2,1,0:T(8,128)(2,1)S(1)} %get-tuple-element.29), channel_id=1, source_target_pairs={{0,1},{1,0},{2,3},{3,2},{4,5},{5,4},{6,7},{7,6},{8,9},{9,8},{10,11... | collective-permute-start | bytes 122888 | tf_op jit(solution)/shard_map/ppermute | solution.py:388
  7.7 10.7 %collective-permute-start.5 = (bf16[9,48,128]{2,1,0:T(8,128)(2,1)S(1)}, bf16[9,48,128]{2,1,0:T(8,128)(2,1)S(1)}, u32[]{:S(2)}, u32[]{:S(2)}) collective-permute-start(bf16[9,48,128]{2,1,0:T(8,128)(2,1)S(1)} %get-tuple-element.33), channel_id=1, source_target_pairs={{0,3},{1,2},{2,1},{3,0},{4,7},{5,6},{6,5},{7,4},{8,11},{9,10},{10,... | collective-permute-start | bytes 331784 | tf_op jit(solution)/shard_map/ppermute | solution.py:388
  11.5 9.5 %collective-permute-start.6 = (bf16[9,48,128]{2,1,0:T(8,128)(2,1)S(1)}, bf16[9,48,128]{2,1,0:T(8,128)(2,1)S(1)}, u32[]{:S(2)}, u32[]{:S(2)}) collective-permute-start(bf16[9,48,128]{2,1,0:T(8,128)(2,1)S(1)} %get-tuple-element.34), channel_id=1, source_target_pairs={{0,2},{1,3},{2,0},{3,1},{4,6},{5,7},{6,4},{7,5},{8,10},{9,11},{10,... | collective-permute-start | bytes 331784 | tf_op jit(solution)/shard_map/ppermute | solution.py:388
  11.5 0.7 %copy-start.7 = (s32[1,1,8]{2,1,0:T(1,128)S(1)}, s32[1,1,8]{2,1,0:T(1,128)}, u32[]{:S(2)}) copy-start(s32[1,1,8]{2,1,0:T(1,128)} %param.11) | copy-start | bytes 100
  11.5 9.4 %collective-permute-start.7 = (bf16[9,48,128]{2,1,0:T(8,128)(2,1)S(1)}, bf16[9,48,128]{2,1,0:T(8,128)(2,1)S(1)}, u32[]{:S(2)}, u32[]{:S(2)}) collective-permute-start(bf16[9,48,128]{2,1,0:T(8,128)(2,1)S(1)} %get-tuple-element.35), channel_id=1, source_target_pairs={{0,1},{1,0},{2,3},{3,2},{4,5},{5,4},{6,7},{7,6},{8,9},{9,8},{10,11... | collective-permute-start | bytes 331784 | tf_op jit(solution)/shard_map/ppermute | solution.py:388
  12.1 0.7 %copy-start.5 = (s32[1,1,8,128]{3,2,1,0:T(8,128)S(1)}, s32[1,1,8,128]{3,2,1,0:T(8,128)}, u32[]{:S(2)}) copy-start(s32[1,1,8,128]{3,2,1,0:T(8,128)} %param.9) | copy-start | bytes 12292
  12.1 0.7 %copy-start.6 = (s32[1,1,8,128]{3,2,1,0:T(8,128)S(1)}, s32[1,1,8,128]{3,2,1,0:T(8,128)}, u32[]{:S(2)}) copy-start(s32[1,1,8,128]{3,2,1,0:T(8,128)} %param.10) | copy-start | bytes 12292
  15.8 8.3 %collective-permute-start.3 = (bf16[4,80,128]{2,1,0:T(8,128)(2,1)S(1)}, bf16[4,80,128]{2,1,0:T(8,128)(2,1)S(1)}, u32[]{:S(2)}, u32[]{:S(2)}) collective-permute-start(bf16[4,80,128]{2,1,0:T(8,128)(2,1)S(1)} %get-tuple-element.31), channel_id=1, source_target_pairs={{0,4},{4,0},{8,12},{12,8},{16,20},{20,16},{24,28},{28,24},{1,5},{5... | collective-permute-start | bytes 245768 | tf_op jit(solution)/shard_map/ppermute | solution.py:388
  15.8 8.2 %collective-permute-start.4 = (bf16[4,80,128]{2,1,0:T(8,128)(2,1)S(1)}, bf16[4,80,128]{2,1,0:T(8,128)(2,1)S(1)}, u32[]{:S(2)}, u32[]{:S(2)}) collective-permute-start(bf16[4,80,128]{2,1,0:T(8,128)(2,1)S(1)} %get-tuple-element.32), channel_id=1, source_target_pairs={{4,8},{12,16},{20,24},{0,28},{8,4},{16,12},{24,20},{28,0},{5,9},{1... | collective-permute-start | bytes 245768 | tf_op jit(solution)/shard_map/ppermute | solution.py:447
  27.1 5.4 %collective-permute-start.8 = (bf16[2,128,128]{2,1,0:T(8,128)(2,1)S(1)}, bf16[2,128,128]{2,1,0:T(8,128)(2,1)S(1)}, u32[]{:S(2)}, u32[]{:S(2)}) collective-permute-start(bf16[2,128,128]{2,1,0:T(8,128)(2,1)S(1)} %get-tuple-element.45), channel_id=1, source_target_pairs={{0,24},{4,28},{8,16},{12,20},{16,8},{20,12},{24,0},{28,4},{1,25},{... | collective-permute-start | bytes 196616 | tf_op jit(solution)/shard_map/ppermute | solution.py:388
  29.6 4.3 %collective-permute-start.9 = (bf16[2,128,128]{2,1,0:T(8,128)(2,1)S(1)}, bf16[2,128,128]{2,1,0:T(8,128)(2,1)S(1)}, u32[]{:S(2)}, u32[]{:S(2)}) collective-permute-start(bf16[2,128,128]{2,1,0:T(8,128)(2,1)S(1)} %get-tuple-element.46), channel_id=1, source_target_pairs={{0,16},{4,20},{8,24},{12,28},{16,0},{20,4},{24,8},{28,12},{1,17},{... | collective-permute-start | bytes 196616 | tf_op jit(solution)/shard_map/ppermute | solution.py:388
  30.1 4.3 %collective-permute-start.10 = (bf16[2,128,128]{2,1,0:T(8,128)(2,1)S(1)}, bf16[2,128,128]{2,1,0:T(8,128)(2,1)S(1)}, u32[]{:S(2)}, u32[]{:S(2)}) collective-permute-start(bf16[2,128,128]{2,1,0:T(8,128)(2,1)S(1)} %get-tuple-element.47), channel_id=1, source_target_pairs={{0,8},{4,12},{8,0},{12,4},{16,24},{20,28},{24,16},{28,20},{1,9},{5... | collective-permute-start | bytes 196616 | tf_op jit(solution)/shard_map/ppermute | solution.py:388
  34.4 1.4 %collective-permute-start.11 = (bf16[4,128,128]{2,1,0:T(8,128)(2,1)S(1)}, bf16[4,128,128]{2,1,0:T(8,128)(2,1)S(1)}, u32[]{:S(2)}, u32[]{:S(2)}) collective-permute-start(bf16[4,128,128]{2,1,0:T(8,128)(2,1)S(1)} %shard_map.100), channel_id=1, source_target_pairs={{0,4},{4,0},{8,12},{12,8},{16,20},{20,16},{24,28},{28,24},{1,5},{5... | collective-permute-start | bytes 393224 | tf_op jit(solution)/shard_map/ppermute | solution.py:388

commit v3 on v2

v3 whole, which is shorter than its diff:
```python
import math

import jax
import jax.numpy as jnp
import numpy as np
from jax import lax
from jax.experimental import pallas as pl
from jax.experimental.pallas import tpu as pltpu
from jax.sharding import PartitionSpec as P

RADIUS = 8
SLOTS = 1024
LANES = 128
BLOCK = 256
TILE = 16

narrow_sigma = (1.0, 2.0, 2.0)
broad_sigma = (1.6, 3.2, 3.2)
contrast = 20.0
epsilon = 1e-06

F32 = jnp.float32
BF16 = jnp.bfloat16


def gauss_taps(sigma, radius):
    weights = [math.exp(-0.5 * (offset / sigma) ** 2) for offset in range(-radius, radius + 1)]
    scale_total = sum(weights)
    return [weight / scale_total for weight in weights]


def taps(along):
    return [
        np.asarray(gauss_taps(sigma[along], RADIUS), np.float32)
        for sigma in (narrow_sigma, broad_sigma)
    ]


def stencil(distance, tap):
    total = jnp.zeros(distance.shape, F32)
    for reach in range(RADIUS + 1):
        total = jnp.where(jnp.abs(distance) == reach, float(tap[RADIUS + reach]), total)
    return total


def split(weight):
    high = weight.astype(BF16).astype(F32)
    return high, (weight - high).astype(BF16).astype(F32)


def grid(rows, columns):
    shape = (rows, columns)
    return [lax.broadcasted_iota(jnp.int32, shape, axis) for axis in range(2)]


def x_weights(wm_ref, ws_ref):
    row, column = grid(LANES, LANES)
    place = row % (2 * RADIUS)
    margin = jnp.where(place < RADIUS, place - RADIUS, place - RADIUS + LANES)
    group = lax.broadcasted_iota(jnp.int32, (LANES, 2 * LANES), 0) // (2 * RADIUS)
    for ref, at in ((wm_ref, row), (ws_ref, margin)):
        whole = jnp.concatenate([stencil(at - column, tap) for tap in taps(2)], axis=1)
        for part, value in enumerate(split(whole)):
            span = slice(part * LANES, (part + 1) * LANES)
            if ref is wm_ref:
                ref[span] = value.astype(BF16)
                continue
            for z in range(ref.shape[0]):
                ref[z, span] = jnp.where(group == z, value, 0.0).astype(BF16)


def y_weights(odd, out_ref):
    rows = out_ref.shape[1]
    out, lane = grid(rows, 4 * rows)
    place, block = lane % rows, lane // rows
    first = jnp.where(odd, place, place + rows - RADIUS)
    second = jnp.where(odd, place + rows - 2 * RADIUS, place - RADIUS)
    at = jnp.where(place < RADIUS, first, jnp.where(place < 2 * RADIUS, second, place - RADIUS))
    for f, tap in enumerate(taps(1)):
        high, low = split(stencil(at - out, tap))
        out_ref[f] = jnp.where(block % 2 == 0, high, low).astype(BF16)


def y_margin_weights(odd, rows, out_ref):
    both = 2 * RADIUS
    row, lane = grid(*out_ref.shape[1:])
    out = row % both
    out = jnp.where(out < RADIUS, out, out + rows - both)
    block, place = lane % (4 * both) // both, lane % both
    low, high = place % RADIUS - RADIUS, place % RADIUS + rows
    near = place < RADIUS
    at = jnp.where(jnp.logical_xor(near, odd), high, low)
    same = row // both == lane // (4 * both)
    for f, tap in enumerate(taps(1)):
        top, rest = split(stencil(at - out, tap))
        value = jnp.where(block % 2 == 0, top, rest)
        out_ref[f] = jnp.where(same, value, 0.0).astype(BF16)


def edge_rows(zlocal):
    return -(-(zlocal + 1) * RADIUS // 16) * 16


def column_tile(source, which):
    at = pl.ds(pl.multiple_of(which * LANES, LANES), LANES)
    return source(at)


def with_margin(source, dest, views, rows):
    lane = lax.broadcasted_iota(jnp.int32, (rows, LANES), 1)
    left = column_tile(source, jnp.maximum(dest - 1, 0))
    right = column_tile(source, jnp.minimum(dest + 1, views - 1))
    lowest = jnp.where(dest > 0, LANES - RADIUS, LANES)
    highest = jnp.where(dest < views - 1, RADIUS, 0)
    margin = jnp.where(lane < highest, right, jnp.where(lane >= lowest, left, 0.0))
    return column_tile(source, dest), margin


def place_margin(margin, z):
    return pltpu.roll(margin, (2 * RADIUS * z + RADIUS) % LANES, 1)


def pack_kernel(shifts, planes_ref, *outs):
    views = len(shifts)
    edges, inner = outs[:views], outs[views:]
    zlocal, rows = planes_ref.shape[:2]
    me = lax.axis_index("view")
    odd = lax.axis_index("bulk") % 2 == 1
    for k, shift in enumerate(shifts):
        groups = []
        packed = None
        for z in range(zlocal):
            main, margin = with_margin(
                lambda at: planes_ref[z, :, at].astype(F32), me ^ shift, views, rows
            )
            groups.append(main)
            placed = place_margin(margin, z)
            packed = placed if packed is None else packed + placed
        groups.append(packed)
        low = [g[:RADIUS] for g in groups]
        high = [g[rows - RADIUS :] for g in groups]
        pad = edges[k].shape[1] - len(groups) * RADIUS
        if pad:
            low.append(jnp.zeros((pad, LANES), F32))
            high.append(jnp.zeros((pad, LANES), F32))
        low, high = jnp.concatenate(low, axis=0), jnp.concatenate(high, axis=0)
        edges[k][0] = jnp.where(odd, low, high).astype(BF16)
        edges[k][1] = jnp.where(odd, high, low).astype(BF16)
        for g, group in enumerate(groups):
            inner[k][g] = group[RADIUS : rows - RADIUS].astype(BF16)


def margin_kernel(*refs):
    *edges, near_ref, far_ref, token_ref = refs
    token_ref[...] = jnp.zeros(token_ref.shape, F32)
    for k, edge in enumerate(edges):
        near_ref[k] = edge[0]
        far_ref[k] = edge[1]


def partner(brick, chip, core):
    return brick ^ jnp.where(brick % 2 == 1, chip[1], chip[0]) ^ core


def prepare_kernel(packed_ref, wm_ref, ws_ref, inside_ref, margin_ref):
    del packed_ref
    odd = lax.axis_index("bulk") % 2 == 1
    x_weights(wm_ref, ws_ref)
    y_weights(odd, inside_ref)
    y_margin_weights(odd, inside_ref.shape[1], margin_ref)


def lists_kernel(chips, token_ref, index_ref, slot_ref, count_ref, column_ref, target_ref):
    del token_ref
    brick = lax.axis_index("bulk")
    wanted = jnp.concatenate(
        [index_ref[pl.ds(partner(brick, c, core), 1), :] for c in chips for core in range(2)],
        axis=0,
    )
    column_ref[...] = jnp.transpose(wanted.astype(F32))
    candidate = lax.broadcasted_iota(jnp.int32, slot_ref.shape, 1)
    counts = jnp.broadcast_to(count_ref[...].astype(F32), (LANES, count_ref.shape[1]))
    counts = jnp.transpose(counts)[:, : slot_ref.shape[1]].astype(jnp.int32)
    target_ref[...] = jnp.where(candidate < counts, slot_ref[...], -1)


def twice(block):
    return jnp.concatenate([block, block], axis=1)


def split_stack(data):
    high = data.astype(BF16)
    low = (data - high.astype(F32)).astype(BF16)
    return [high, high, low, low]


def z_pass(load, planes_z):
    data = [[load(f, z) for z in range(planes_z)] for f in range(2)]
    z_taps = taps(0)
    scale = (contrast, -contrast)
    out = []
    for z in range(planes_z):
        total = None
        for f in range(2):
            for reach in range(RADIUS + 1):
                weight = float(scale[f] * z_taps[f][RADIUS + reach])
                near = [z] if reach == 0 else [z - reach, z + reach]
                sides = [data[f][q] for q in near if 0 <= q < planes_z]
                if not sides:
                    continue
                both = sides[0] if len(sides) == 1 else sides[0] + sides[1]
                term = weight * both
                total = term if total is None else total + term
        out.append(total)
    return out


def plane_passes(edges, inner, wm_ref, ws_ref, wy_ref, write):
    count = len(edges)
    zlocal, rows = inner[0].shape[0] - 1, wy_ref.shape[1]
    small = [[e[part].astype(F32) for part in range(2)] for e in edges]

    def rows_of(k, g):
        top = [s[g * RADIUS : (g + 1) * RADIUS] for s in small[k]]
        return [jnp.concatenate(top, axis=0).astype(BF16), inner[k][g]]

    def stacked(z):
        return twice(jnp.concatenate([p for k in range(count) for p in rows_of(k, z)], axis=0))

    margins = stacked(zlocal)

    def x_pass(z):
        main = jnp.dot(stacked(z), wm_ref[...], preferred_element_type=F32)
        return main + jnp.dot(margins, ws_ref[z], preferred_element_type=F32)

    for z in range(0, zlocal, 2):
        pair = [x_pass(z), x_pass(z + 1)]
        for k in range(count):
            for f in range(2):
                data = jnp.concatenate(
                    [
                        p[k * rows : (k + 1) * rows, f * LANES : (f + 1) * LANES]
                        for p in pair
                    ],
                    axis=1,
                )
                operand = jnp.concatenate(split_stack(data), axis=0)
                out = jnp.dot(wy_ref[f], operand, preferred_element_type=F32)
                write(k, z, f, out[:, :LANES])
                write(k, z + 1, f, out[:, LANES:])


def early_kernel(token_ref, edge_ref, inner_ref, wm_ref, ws_ref, wy_ref, out_ref, _):
    del token_ref

    def write(k, z, f, value):
        del k
        out_ref[f, z] = value

    plane_passes([edge_ref], [inner_ref], wm_ref, ws_ref, wy_ref, write)


def late_kernel(shifts, target_ref, own_ref, *refs):
    del target_ref
    *refs, wm_ref, ws_ref, wy_ref, fields, _ = refs
    count = len(refs) // 2
    zlocal = own_ref.shape[1]
    me = lax.axis_index("view")
    for f in range(2):
        fields[f, pl.ds(me * zlocal, zlocal)] = own_ref[f]

    def write(k, z, f, value):
        fields[f, (me ^ shifts[k]) * zlocal + z] = value

    plane_passes(refs[:count], refs[count:], wm_ref, ws_ref, wy_ref, write)


def border_kernel(shifts, target_ref, near_ref, far_ref, wm_ref, ws_ref, wy_ref, out_ref, _):
    del target_ref
    views = len(shifts)
    halo = (near_ref, far_ref)
    zlocal = out_ref.shape[1] // views
    both = 2 * RADIUS
    me = lax.axis_index("view")
    brick = lax.axis_index("bulk")
    ends = (brick == 0) | (brick == lax.axis_size("bulk") - 1)

    def margin(part, k):
        data = halo[part][k].astype(F32)
        return jnp.where(ends, 0.0, data) if part == 1 else data

    small = [[margin(part, k) for part in range(2)] for k in range(views)]

    def rows_of(k, g):
        return [s[g * RADIUS : (g + 1) * RADIUS] for s in small[k]]

    main = [p for k in range(views) for z in range(zlocal) for p in rows_of(k, z)]
    side = [p for k in range(views) for p in rows_of(k, zlocal)]
    main = twice(jnp.concatenate(main, axis=0).astype(BF16))
    side = twice(jnp.concatenate(side, axis=0).astype(BF16))
    main = jnp.dot(main, wm_ref[...], preferred_element_type=F32)
    side = [jnp.dot(side, ws_ref[z], preferred_element_type=F32) for z in range(zlocal)]
    for k in range(views):
        smooth = [
            main[(k * zlocal + z) * both : (k * zlocal + z + 1) * both]
            + side[z][k * both : (k + 1) * both]
            for z in range(zlocal)
        ]
        at = (me ^ shifts[k]) * zlocal
        for f in range(2):
            parts = []
            for z in range(0, zlocal, 2):
                parts += split_stack(
                    jnp.concatenate(
                        [p[:, f * LANES : (f + 1) * LANES] for p in smooth[z : z + 2]], axis=1
                    )
                )
            operand = jnp.concatenate(parts, axis=0)
            out = jnp.dot(wy_ref[f], operand, preferred_element_type=F32)
            for z in range(zlocal):
                row, lane = z // 2 * both, z % 2 * LANES
                out_ref[f, at + z] = out[row : row + both, lane : lane + LANES]


def filter_kernel(chips, fields_ref, border_ref, column_ref, fields, dog_hbm, *refs):
    del fields_ref
    chosen, (dog_ref, written) = refs[: len(chips)], refs[len(chips) :]
    planes_z, rows = dog_ref.shape[:2]
    for f in range(2):
        fields[f, :, :RADIUS] += border_ref[f, :, :RADIUS]
        fields[f, :, rows - RADIUS :] += border_ref[f, :, RADIUS:]

    def tile(step, carry):
        at = pl.ds(pl.multiple_of(step * TILE, TILE), TILE)
        done = z_pass(lambda f, z: fields[f, z, at, :], planes_z)
        for z in range(planes_z):
            dog_ref[z, at, :] = done[z].astype(BF16)
        return carry

    lax.fori_loop(0, rows // TILE, tile, 0)

    parts = written.shape[0]
    copies = []
    for part in range(parts):
        span = pl.ds(part * (planes_z // parts), planes_z // parts)
        copies.append(
            pltpu.make_async_copy(dog_ref.at[span], dog_hbm.at[span], written.at[part])
        )
        copies[-1].start()

    half = planes_z * rows // 2
    flat = dog_ref[...].reshape(2 * half, LANES)
    flat = jnp.concatenate([flat[:half], flat[half:]], axis=1)
    columns = column_ref[...]
    offered = columns.shape[0]
    lane = lax.broadcasted_iota(jnp.int32, (offered, BLOCK), 1).astype(F32).astype(BF16)
    for m in range(2 * len(chips)):
        column = columns[:, m : m + 1]
        later = column >= half
        column = jnp.where(later, column - half, column)
        upper = jnp.floor(column * (1.0 / BLOCK))
        lower = column - BLOCK * upper
        onehot = []
        for j in range(half // BLOCK):
            here = jnp.where(upper == j, lower, -1.0).astype(BF16)
            onehot.append(jnp.where(lane == here, 1.0, 0.0).astype(BF16))
        onehot = jnp.concatenate(onehot, axis=1)
        picked = jnp.dot(onehot, flat, preferred_element_type=F32)
        picked = jnp.where(later, picked[:, LANES:], picked[:, :LANES])
        chosen[m // 2][m % 2] = picked.astype(BF16)
    for copy in copies:
        copy.wait()


def forward_kernel(target_ref, *refs):
    *rows, out_ref, _ = refs
    del target_ref
    for c, row in enumerate(rows):
        out_ref[c] = row[1]


def merge_rows(chips, core, rows, target_ref, slots, emit):
    owner = lax.axis_index("bulk")
    target = jnp.concatenate(
        [target_ref[pl.ds(partner(owner ^ core, c, 0), 1), :] for c in chips], axis=1
    )
    received = jnp.concatenate(rows, axis=0)
    upper, lower = target >> 8, (target & (BLOCK - 1)).astype(F32)
    place = lax.broadcasted_iota(jnp.int32, (BLOCK, target.shape[1]), 0).astype(F32).astype(BF16)
    for block in range(slots // BLOCK):
        wanted = jnp.where(upper == block, lower, -1.0).astype(BF16)
        onehot = jnp.where(place == wanted, 1.0, 0.0).astype(BF16)
        emit(block, jnp.dot(onehot, received, preferred_element_type=F32))


def merge_kernel(chips, target_ref, *refs):
    *rows, out_ref = refs

    def emit(block, sums):
        out_ref[block * BLOCK : (block + 1) * BLOCK] = sums

    merge_rows(chips, 0, [r[0] for r in rows], target_ref, out_ref.shape[0], emit)


def finish_kernel(chips, passed_ref, target_ref, sums_ref, out_hbm, out_ref, written):
    slots = out_ref.shape[0]
    copies = []

    def emit(block, sums):
        span = pl.ds(block * BLOCK, BLOCK)
        summed = sums_ref[span] + sums
        scale = lax.rsqrt(jnp.mean(summed * summed, axis=-1, keepdims=True) + epsilon)
        out_ref[span] = summed * scale
        copies.append(
            pltpu.make_async_copy(out_ref.at[span], out_hbm.at[span], written.at[block])
        )
        copies[-1].start()

    rows = [passed_ref[c] for c in range(len(chips))]
    merge_rows(chips, 1, rows, target_ref, slots, emit)
    for copy in copies:
        copy.wait()


def swap(block, axis, distance):
    if distance == 0:
        return block
    count = lax.axis_size(axis)
    return lax.ppermute(block, axis, [(i, i ^ distance) for i in range(count)])


def local(planes, cand_index, recv_slot, recv_count):
    views = lax.axis_size("view")
    bricks = lax.axis_size("bulk")
    zlocal, rows, width = planes.shape
    planes_z = zlocal * views
    owners, offered = cand_index.shape[2:]
    vmem = pl.BlockSpec(memory_space=pltpu.VMEM)
    hbm = pl.BlockSpec(memory_space=pltpu.HBM)
    params = pltpu.CompilerParams(vmem_limit_bytes=20 * 1024 * 1024)
    edge = jax.ShapeDtypeStruct((2, edge_rows(zlocal), LANES), BF16)
    body = jax.ShapeDtypeStruct((zlocal + 1, rows - 2 * RADIUS, LANES), BF16)
    halo = jax.ShapeDtypeStruct((views, edge_rows(zlocal), LANES), BF16)
    targets = jax.ShapeDtypeStruct((owners, offered), jnp.int32)
    shifts = list(range(views - 1, -1, -1))
    chips = list(range(owners - 2, -1, -2))
    chips = list(zip(chips, chips[:1] + chips[-2:0:-1] + chips[-1:]))

    packed = pl.pallas_call(
        lambda *refs: pack_kernel(shifts, *refs),
        out_shape=[edge] * views + [body] * views,
        in_specs=[vmem],
        out_specs=[vmem] * (2 * views),
        compiler_params=params,
    )(planes)
    edges = {k: swap(e, "view", k) for e, k in zip(packed[:views], shifts)}
    inner = {k: swap(e, "view", k) for e, k in zip(packed[views:], shifts)}
    edge_order = [2, 3, 1, 0] if views == 4 else shifts
    inner_order = [2, 3, 1] if views == 4 else shifts[:-1]

    pairs = zlocal // 2
    main_w, side_w, inside_w, margin_w = pl.pallas_call(
        prepare_kernel,
        out_shape=[
            jax.ShapeDtypeStruct((2 * LANES, 2 * LANES), BF16),
            jax.ShapeDtypeStruct((zlocal, 2 * LANES, 2 * LANES), BF16),
            jax.ShapeDtypeStruct((2, rows, 4 * rows), BF16),
            jax.ShapeDtypeStruct((2, 2 * RADIUS * pairs, 8 * RADIUS * pairs), BF16),
        ],
        in_specs=[vmem],
        out_specs=[vmem] * 4,
        compiler_params=params,
    )(edges[0])
    token = jax.ShapeDtypeStruct((RADIUS, LANES), F32)
    near, far, passed = pl.pallas_call(
        margin_kernel,
        out_shape=[halo] * 2 + [token],
        in_specs=[vmem] * views,
        out_specs=[vmem] * 3,
        compiler_params=params,
    )(*[edges[k] for k in edge_order])
    own, passed = pl.pallas_call(
        early_kernel,
        out_shape=[jax.ShapeDtypeStruct((2, zlocal, rows, LANES), F32), token],
        in_specs=[vmem] * 6,
        out_specs=[vmem] * 2,
        input_output_aliases={0: 1},
        compiler_params=params,
    )(passed, edges[0], inner[0], main_w, side_w, inside_w)
    columns, target = pl.pallas_call(
        lambda *refs: lists_kernel(chips, *refs),
        out_shape=[jax.ShapeDtypeStruct((offered, owners), F32), targets],
        in_specs=[vmem] * 4,
        out_specs=[vmem] * 2,
        compiler_params=params,
    )(
        passed,
        cand_index.reshape(owners, offered),
        recv_slot.reshape(owners, offered),
        recv_count.reshape(1, owners),
    )
    far_pairs = [(i, i + 1) for i in range(1, bricks - 1, 2)] + [(0, bricks - 1)]
    far_pairs = far_pairs + [(target, source) for source, target in far_pairs]
    far = lax.ppermute(far, "bulk", far_pairs)
    near = swap(near, "bulk", 1)

    whole = jax.ShapeDtypeStruct((2, planes_z, rows, LANES), F32)
    fields, target = pl.pallas_call(
        lambda *refs: late_kernel(inner_order, *refs),
        out_shape=[whole, targets],
        in_specs=[vmem] * (2 * views + 3),
        out_specs=[vmem] * 2,
        input_output_aliases={0: 1},
        compiler_params=params,
    )(
        target,
        own,
        *[edges[k] for k in inner_order],
        *[inner[k] for k in inner_order],
        main_w,
        side_w,
        inside_w,
    )
    border, target = pl.pallas_call(
        lambda *refs: border_kernel(edge_order, *refs),
        out_shape=[jax.ShapeDtypeStruct((2, planes_z, 2 * RADIUS, LANES), F32), targets],
        in_specs=[vmem] * 6,
        out_specs=[vmem] * 2,
        input_output_aliases={0: 1},
        compiler_params=params,
    )(target, near, far, main_w, side_w, margin_w)

    offers = jax.ShapeDtypeStruct((2, offered, LANES), BF16)
    _, dog, *chosen = pl.pallas_call(
        lambda *refs: filter_kernel(chips, *refs),
        out_shape=[whole, jax.ShapeDtypeStruct((planes_z, rows, LANES), BF16)]
        + [offers] * len(chips),
        in_specs=[vmem] * 3,
        out_specs=[vmem, hbm] + [vmem] * len(chips),
        input_output_aliases={0: 0},
        scratch_shapes=[
            pltpu.VMEM((planes_z, rows, LANES), BF16),
            pltpu.SemaphoreType.DMA((8,)),
        ],
        compiler_params=params,
    )(fields, border, columns)
    received = [
        lax.ppermute(c, "bulk", [(i, i ^ chip[i % 2]) for i in range(bricks)]) if max(chip) else c
        for c, chip in zip(chosen, chips)
    ]
    passed, target = pl.pallas_call(
        forward_kernel,
        out_shape=[jax.ShapeDtypeStruct((len(chips), offered, LANES), BF16), targets],
        in_specs=[vmem] * (len(chips) + 1),
        out_specs=[vmem] * 2,
        input_output_aliases={0: 1},
        compiler_params=params,
    )(target, *received)
    passed = swap(passed, "bulk", 1)
    sums = pl.pallas_call(
        lambda *refs: merge_kernel(chips, *refs),
        out_shape=jax.ShapeDtypeStruct((SLOTS, LANES), F32),
        in_specs=[vmem] * (len(chips) + 1),
        out_specs=vmem,
        compiler_params=params,
    )(target, *received)
    descriptors = pl.pallas_call(
        lambda *refs: finish_kernel(chips, *refs),
        out_shape=jax.ShapeDtypeStruct((SLOTS, LANES), F32),
        in_specs=[vmem] * 3,
        out_specs=hbm,
        scratch_shapes=[
            pltpu.VMEM((SLOTS, LANES), F32),
            pltpu.SemaphoreType.DMA((SLOTS // BLOCK,)),
        ],
        compiler_params=params,
    )(passed, target, sums)
    return (dog, descriptors.reshape(1, 1, SLOTS, LANES))


def solution(mesh):
    in_specs = (
        P("view", "bulk", None),
        P("bulk", "view", None, None),
        P("bulk", "view", None, None),
        P("bulk", "view", None),
    )
    out_specs = (P(None, "bulk", "view"), P("bulk", "view", None, None))
    return jax.shard_map(local, mesh=mesh, in_specs=in_specs, out_specs=out_specs, check_vma=False)
```

time: 37.8 us -> 35.5 us (0.939)
  waiting for transfers between devices: 10.4 us -> 7.8 us
  Pallas kernels: 8.3 us -> 9.71 us
  local copies, waits for them, and re-layouts: 1.75 us -> 1.05 us
    ppermute x11 -> x8, waiting for transfers between devices: 10.4 us -> 4.06 us  [swap(): return lax.ppermute(block, axis, [(i, i ^ distance) for i in range(count)])]
    ppermute x11 -> x8, starting transfers between devices: 13.8 us -> 9.98 us  [swap(): return lax.ppermute(block, axis, [(i, i ^ distance) for i in range(count)])]
    ppermute x0 -> x3, waiting for transfers between devices: none -> 3.73 us  [local(): lax.ppermute(c, 'bulk', [(i, i ^ chip[i % 2]) for i in range(bricks)])]
    ppermute x0 -> x3, starting transfers between devices: none -> 3.55 us  [local(): lax.ppermute(c, 'bulk', [(i, i ^ chip[i % 2]) for i in range(bricks)])]
    pallas_call x5 -> x9, Pallas kernels: 6.28 us -> 8.92 us  [the longest x1 3.38 us: local(): pl.pallas_call(lambda *refs: filter_kernel(chips, *refs), out_shape=[whol...]
    pallas_call x1, Pallas kernels: 1.73 us -> 0.51 us  [local(): pl.pallas_call(lambda *refs: merge_kernel(chips, *refs), out_shape=jax.Sh...]
    unnamed x16 -> x8, local copies, waits for them, and re-layouts: 1.67 us -> 1.05 us
  transfers between devices with their start and end apart: 12 -> 12, of which waited for: 6 -> 7; matrix products, arithmetic and copies ran while one was open for 0% -> 0% of each run, Pallas kernels for 9% -> 11%
where the time goes in v3:
time: 35.5 us; the launch traced here: 35.4 us
  starting transfers between devices  16.1 us (45%)
  Pallas kernels  9.71 us (27%)
  waiting for transfers between devices  7.8 us (22%)
  local copies, waits for them, and re-layouts  1.05 us (3%)
  between operations  0.75 us (2%)
    ppermute x8, starting transfers between devices, swap(): return lax.ppermute(block, axis, [(i, i ^ distance) for i in range(count)])  9.98 us
    ppermute x8, waiting for transfers between devices, swap(): return lax.ppermute(block, axis, [(i, i ^ distance) for i in range(count)])  4.06 us
    ppermute x3, waiting for transfers between devices, local(): lax.ppermute(c, 'bulk', [(i, i ^ chip[i % 2]) for i in range(bricks)])  3.73 us
    ppermute x3, starting transfers between devices, local(): lax.ppermute(c, 'bulk', [(i, i ^ chip[i % 2]) for i in range(bricks)])  3.55 us
    pallas_call x1, Pallas kernels, local(): pl.pallas_call(lambda *refs: filter_kernel(chips, *refs), out_shape=[whol...  3.38 us
    ppermute x1, starting transfers between devices, local(): far = lax.ppermute(far, 'bulk', far_pairs)  2.55 us
    pallas_call x1, Pallas kernels, local(): pl.pallas_call(lambda *refs: late_kernel(inner_order, *refs), out_shape=[...  1.6 us
    pallas_call x1, Pallas kernels, local(): pl.pallas_call(lambda *refs: finish_kernel(chips, *refs), out_shape=jax.S...  1.33 us
  transfers between devices with their start and end apart: 12, of which 7 were waited for; matrix products, arithmetic and copies ran while one was open for 0% of the time, Pallas kernels for 11%

profile of v3, /device:TPU:0, one launch (start us, length us, event | category | flops | bytes accessed | tf_op | source)
XLA Modules:
  0.0 35.4 jit_solution(6192395305777344773)
XLA Ops:
  0.6 0.0 copy-start
  0.6 1.0 %copy-done = bf16[8,64,512]{2,1,0:T(8,128)(2,1)S(1)} copy-done((bf16[8,64,512]{2,1,0:T(8,128)(2,1)S(1)}, bf16[8,64,512]{2,1,0:T(8,128)(2,1)}, u32[]{:S(2)}) %copy-start) | copy-done | bytes 524312
  1.7 0.0 copy-start.1
  1.7 0.0 copy-start.2
  1.7 0.0 copy-start.3
  1.7 0.3 shard_map.59
  2.0 4.1 %collective-permute-start = (bf16[2,80,128]{2,1,0:T(8,128)(2,1)S(1)}, bf16[2,80,128]{2,1,0:T(8,128)(2,1)S(1)}, u32[]{:S(2)}, u32[]{:S(2)}) collective-permute-start(bf16[2,80,128]{2,1,0:T(8,128)(2,1)S(1)} %get-tuple-element.32), channel_id=1, source_target_pairs={{0,2},{1,3},{2,0},{3,1},{4,6},{5,7},{6,4},{7,5},{8,10},{9,11},{10,... | collective-permute-start | bytes 122888 | tf_op jit(solution)/shard_map/ppermute | solution.py:429
  6.1 1.3 %collective-permute-start.1 = (bf16[2,80,128]{2,1,0:T(8,128)(2,1)S(1)}, bf16[2,80,128]{2,1,0:T(8,128)(2,1)S(1)}, u32[]{:S(2)}, u32[]{:S(2)}) collective-permute-start(bf16[2,80,128]{2,1,0:T(8,128)(2,1)S(1)} %get-tuple-element.33), channel_id=1, source_target_pairs={{0,3},{1,2},{2,1},{3,0},{4,7},{5,6},{6,5},{7,4},{8,11},{9,10},{10,... | collective-permute-start | bytes 122888 | tf_op jit(solution)/shard_map/ppermute | solution.py:429
  7.4 0.2 collective-permute-start.2
  7.6 2.8 %collective-permute-start.3 = (bf16[9,48,128]{2,1,0:T(8,128)(2,1)S(1)}, bf16[9,48,128]{2,1,0:T(8,128)(2,1)S(1)}, u32[]{:S(2)}, u32[]{:S(2)}) collective-permute-start(bf16[9,48,128]{2,1,0:T(8,128)(2,1)S(1)} %get-tuple-element.44), channel_id=1, source_target_pairs={{0,2},{1,3},{2,0},{3,1},{4,6},{5,7},{6,4},{7,5},{8,10},{9,11},{10,... | collective-permute-start | bytes 331784 | tf_op jit(solution)/shard_map/ppermute | solution.py:429
  10.4 1.3 %collective-permute-start.4 = (bf16[9,48,128]{2,1,0:T(8,128)(2,1)S(1)}, bf16[9,48,128]{2,1,0:T(8,128)(2,1)S(1)}, u32[]{:S(2)}, u32[]{:S(2)}) collective-permute-start(bf16[9,48,128]{2,1,0:T(8,128)(2,1)S(1)} %get-tuple-element.45), channel_id=1, source_target_pairs={{0,3},{1,2},{2,1},{3,0},{4,7},{5,6},{6,5},{7,4},{8,11},{9,10},{10,... | collective-permute-start | bytes 331784 | tf_op jit(solution)/shard_map/ppermute | solution.py:429
  11.8 0.0 collective-permute-done.refs_0_.refs_2_
  11.8 0.0 collective-permute-start.5
  11.8 0.6 %collective-permute-done.1.refs_1_.refs_3_ = bf16[2,80,128]{2,1,0:T(8,128)(2,1)S(1)} collective-permute-done((bf16[2,80,128]{2,1,0:T(8,128)(2,1)S(1)}, bf16[2,80,128]{2,1,0:T(8,128)(2,1)S(1)}, u32[]{:S(2)}, u32[]{:S(2)}) %collective-permute-start.1) | collective-permute-done | bytes 40992 | tf_op jit(solution)/shard_map/ppermute | solution.py:429
  12.4 0.0 collective-permute-done.2.refs_2_.refs_4_
  12.4 0.1 collective-permute-start.6
  12.5 2.5 %collective-permute-start.7 = (bf16[4,80,128]{2,1,0:T(8,128)(2,1)S(1)}, bf16[4,80,128]{2,1,0:T(8,128)(2,1)S(1)}, u32[]{:S(2)}, u32[]{:S(2)}) collective-permute-start(bf16[4,80,128]{2,1,0:T(8,128)(2,1)S(1)} %get-tuple-element.50), channel_id=1, source_target_pairs={{4,8},{12,16},{20,24},{0,28},{8,4},{16,12},{24,20},{28,0},{5,9},{1... | collective-permute-start | bytes 245768 | tf_op jit(solution)/shard_map/ppermute | solution.py:504
  15.0 0.5 %shard_map.61 = (bf16[256,256]{1,0:T(8,128)(2,1)S(1)}, bf16[8,256,256]{2,1,0:T(8,128)(2,1)S(1)}, bf16[2,64,256]{2,1,0:T(8,128)(2,1)S(1)}, bf16[2,64,256]{2,1,0:T(8,128)(2,1)S(1)}) custom-call(bf16[2,80,128]{2,1,0:T(8,128)(2,1)S(1)} %get-tuple-element.35.refs_3_.packed_ref.edge_ref), custom_call_target="tpu_custom_call" | custom-call | tf_op jit(solution)/shard_map/pallas_call | solution.py:462
  15.5 1.1 %shard_map.62 = (f32[2,8,64,128]{3,2,1,0:T(8,128)S(1)}, f32[8,128]{1,0:T(8,128)S(1)}) custom-call(f32[8,128]{1,0:T(8,128)S(1)} %get-tuple-element.36.token_ref, bf16[2,80,128]{2,1,0:T(8,128)(2,1)S(1)} %get-tuple-element.35.refs_3_.packed_ref.edge_ref, bf16[9,48,128]{2,1,0:T(8,128)(2,1)S(1)} %get-tuple-element.37.inner_ref, ...), custom_call_target="tpu_custom_call", output_to_operand_aliasing={{1}: (0, {})} | custom-call | tf_op jit(solution)/shard_map/pallas_call | solution.py:482
  16.7 0.0 copy-done.1
  16.7 0.0 copy-done.2
  16.7 0.0 copy-done.3
  16.7 0.1 shard_map.63
  16.8 2.3 %collective-permute-done.3.refs_5_ = bf16[9,48,128]{2,1,0:T(8,128)(2,1)S(1)} collective-permute-done((bf16[9,48,128]{2,1,0:T(8,128)(2,1)S(1)}, bf16[9,48,128]{2,1,0:T(8,128)(2,1)S(1)}, u32[]{:S(2)}, u32[]{:S(2)}) %collective-permute-start.3) | collective-permute-done | bytes 110624 | tf_op jit(solution)/shard_map/ppermute | solution.py:429
  19.1 0.0 collective-permute-done.4.refs_6_
  19.1 0.3 collective-permute-done.5.refs_7_
  19.4 1.6 %shard_map.64 = (f32[2,32,64,128]{3,2,1,0:T(8,128)S(1)}, s32[8,128]{1,0:T(8,128)S(1)}) custom-call(s32[8,128]{1,0:T(8,128)S(1)} %get-tuple-element.42.refs_0_, f32[2,8,64,128]{3,2,1,0:T(8,128)S(1)} %get-tuple-element.43.refs_1_, bf16[2,80,128]{2,1,0:T(8,128)(2,1)S(1)} %collective-permute-done.refs_0_.refs_2_, ...), custom_call_target="tpu_custom_call", output_to_operand_aliasing={{1}: (0, {})} | custom-call | tf_op jit(solution)/shard_map/pallas_call | solution.py:508
  21.1 0.0 collective-permute-done.6.refs_1_
  21.1 0.0 collective-permute-done.7.refs_2_
  21.1 0.9 %shard_map.65 = (f32[2,32,16,128]{3,2,1,0:T(8,128)S(1)}, s32[8,128]{1,0:T(8,128)S(1)}) custom-call(s32[8,128]{1,0:T(8,128)S(1)} %get-tuple-element.48.refs_0_, bf16[4,80,128]{2,1,0:T(8,128)(2,1)S(1)} %collective-permute-done.6.refs_1_, bf16[4,80,128]{2,1,0:T(8,128)(2,1)S(1)} %collective-permute-done.7.refs_2_, ...), custom_call_target="tpu_custom_call", output_to_operand_aliasing={{1}: (0, {})} | custom-call | tf_op jit(solution)/shard_map/pallas_call | solution.py:524
  22.0 3.4 %shard_map.66 = (f32[2,32,64,128]{3,2,1,0:T(8,128)S(1)}, bf16[32,64,128]{2,1,0:T(8,128)(2,1)}, bf16[2,128,128]{2,1,0:T(8,128)(2,1)S(1)}, bf16[2,128,128]{2,1,0:T...) custom-call(f32[2,32,64,128]{3,2,1,0:T(8,128)S(1)} %get-tuple-elemen, ...), custom_call_target="tpu_custom_call", output_to_operand_aliasing={{0}: (0, {})} | custom-call | tf_op jit(solution)/shard_map/pallas_call | solution.py:534
  25.3 2.5 %collective-permute-start.8 = (bf16[2,128,128]{2,1,0:T(8,128)(2,1)S(1)}, bf16[2,128,128]{2,1,0:T(8,128)(2,1)S(1)}, u32[]{:S(2)}, u32[]{:S(2)}) collective-permute-start(bf16[2,128,128]{2,1,0:T(8,128)(2,1)S(1)} %get-tuple-element.56), channel_id=1, source_target_pairs={{0,24},{4,28},{8,16},{12,20},{16,8},{20,12},{24,0},{28,4},{1,25},{... | collective-permute-start | bytes 196616 | tf_op jit(solution)/shard_map/ppermute | solution.py:548
  27.9 0.5 %collective-permute-start.9 = (bf16[2,128,128]{2,1,0:T(8,128)(2,1)S(1)}, bf16[2,128,128]{2,1,0:T(8,128)(2,1)S(1)}, u32[]{:S(2)}, u32[]{:S(2)}) collective-permute-start(bf16[2,128,128]{2,1,0:T(8,128)(2,1)S(1)} %get-tuple-element.57), channel_id=1, source_target_pairs={{0,16},{4,12},{8,24},{12,4},{16,0},{20,28},{24,8},{28,20},{1,17},{... | collective-permute-start | bytes 196616 | tf_op jit(solution)/shard_map/ppermute | solution.py:548
  28.4 0.5 %collective-permute-start.10 = (bf16[2,128,128]{2,1,0:T(8,128)(2,1)S(1)}, bf16[2,128,128]{2,1,0:T(8,128)(2,1)S(1)}, u32[]{:S(2)}, u32[]{:S(2)}) collective-permute-start(bf16[2,128,128]{2,1,0:T(8,128)(2,1)S(1)} %get-tuple-element.58), channel_id=1, source_target_pairs={{0,8},{4,20},{8,0},{12,28},{16,24},{20,4},{24,16},{28,12},{1,9},{5... | collective-permute-start | bytes 196616 | tf_op jit(solution)/shard_map/ppermute | solution.py:548
  28.9 1.7 %collective-permute-done.8.refs_0_.refs_1_ = bf16[2,128,128]{2,1,0:T(8,128)(2,1)S(1)} collective-permute-done((bf16[2,128,128]{2,1,0:T(8,128)(2,1)S(1)}, bf16[2,128,128]{2,1,0:T(8,128)(2,1)S(1)}, u32[]{:S(2)}, u32[]{:S(2)}) %collective-permute-start.8) | collective-permute-done | bytes 65568 | tf_op jit(solution)/shard_map/ppermute | solution.py:548
  30.6 1.5 %collective-permute-done.9.refs_1_.refs_2_ = bf16[2,128,128]{2,1,0:T(8,128)(2,1)S(1)} collective-permute-done((bf16[2,128,128]{2,1,0:T(8,128)(2,1)S(1)}, bf16[2,128,128]{2,1,0:T(8,128)(2,1)S(1)}, u32[]{:S(2)}, u32[]{:S(2)}) %collective-permute-start.9) | collective-permute-done | bytes 65568 | tf_op jit(solution)/shard_map/ppermute | solution.py:548
  32.1 0.5 %collective-permute-done.10.refs_2_.refs_3_ = bf16[2,128,128]{2,1,0:T(8,128)(2,1)S(1)} collective-permute-done((bf16[2,128,128]{2,1,0:T(8,128)(2,1)S(1)}, bf16[2,128,128]{2,1,0:T(8,128)(2,1)S(1)}, u32[]{:S(2)}, u32[]{:S(2)}) %collective-permute-start.10) | collective-permute-done | bytes 65568 | tf_op jit(solution)/shard_map/ppermute | solution.py:548
  32.6 0.1 collective-permute-start.11
  32.7 0.5 %shard_map.68.refs_2_ = f32[1024,128]{1,0:T(8,128)S(1)} custom-call(s32[8,128]{1,0:T(8,128)S(1)} %get-tuple-element.61.refs_0_.refs_1_, bf16[2,128,128]{2,1,0:T(8,128)(2,1)S(1)} %collective-permute-done.8.refs_0_.refs_1_, bf16[2,128,128]{2,1,0:T(8,128)(2,1)S(1)} %collective-permute-done.9.refs_1_.refs_2_, ...), custom_call_target="tpu_custom_call" | custom-call | tf_op jit(solution)/shard_map/pallas_call | solution.py:560
  33.2 0.8 %collective-permute-done.11.refs_0_ = bf16[4,128,128]{2,1,0:T(8,128)(2,1)S(1)} collective-permute-done((bf16[4,128,128]{2,1,0:T(8,128)(2,1)S(1)}, bf16[4,128,128]{2,1,0:T(8,128)(2,1)S(1)}, u32[]{:S(2)}, u32[]{:S(2)}) %collective-permute-start.11) | collective-permute-done | bytes 131104 | tf_op jit(solution)/shard_map/ppermute | solution.py:429
  34.1 1.3 %shard_map.69 = f32[1024,128]{1,0:T(8,128)} custom-call(bf16[4,128,128]{2,1,0:T(8,128)(2,1)S(1)} %collective-permute-done.11.refs_0_, s32[8,128]{1,0:T(8,128)S(1)} %get-tuple-element.61.refs_0_.refs_1_, f32[1024,128]{1,0:T(8,128)S(1)} %shard_map.68.refs_2_), custom_call_target="tpu_custom_call" | custom-call | tf_op jit(solution)/shard_map/pallas_call | solution.py:567
  (2 shorter events, 0.0 us)
Async XLA Ops:
  0.6 1.0 %copy-start = (bf16[8,64,512]{2,1,0:T(8,128)(2,1)S(1)}, bf16[8,64,512]{2,1,0:T(8,128)(2,1)}, u32[]{:S(2)}) copy-start(bf16[8,64,512]{2,1,0:T(8,128)(2,1)} %refs_0_.1) | copy-start | bytes 1572868
  1.7 15.0 %copy-start.1 = (s32[1,1,8,128]{3,2,1,0:T(8,128)S(1)}, s32[1,1,8,128]{3,2,1,0:T(8,128)}, u32[]{:S(2)}) copy-start(s32[1,1,8,128]{3,2,1,0:T(8,128)} %param.5) | copy-start | bytes 12292
  1.7 15.0 %copy-start.2 = (s32[1,1,8,128]{3,2,1,0:T(8,128)S(1)}, s32[1,1,8,128]{3,2,1,0:T(8,128)}, u32[]{:S(2)}) copy-start(s32[1,1,8,128]{3,2,1,0:T(8,128)} %param.6) | copy-start | bytes 12292
  1.7 15.0 %copy-start.3 = (s32[1,1,8]{2,1,0:T(1,128)S(1)}, s32[1,1,8]{2,1,0:T(1,128)}, u32[]{:S(2)}) copy-start(s32[1,1,8]{2,1,0:T(1,128)} %param.7) | copy-start | bytes 100
  2.0 9.8 %collective-permute-start = (bf16[2,80,128]{2,1,0:T(8,128)(2,1)S(1)}, bf16[2,80,128]{2,1,0:T(8,128)(2,1)S(1)}, u32[]{:S(2)}, u32[]{:S(2)}) collective-permute-start(bf16[2,80,128]{2,1,0:T(8,128)(2,1)S(1)} %get-tuple-element.32), channel_id=1, source_target_pairs={{0,2},{1,3},{2,0},{3,1},{4,6},{5,7},{6,4},{7,5},{8,10},{9,11},{10,... | collective-permute-start | bytes 122888 | tf_op jit(solution)/shard_map/ppermute | solution.py:429
  6.1 6.3 %collective-permute-start.1 = (bf16[2,80,128]{2,1,0:T(8,128)(2,1)S(1)}, bf16[2,80,128]{2,1,0:T(8,128)(2,1)S(1)}, u32[]{:S(2)}, u32[]{:S(2)}) collective-permute-start(bf16[2,80,128]{2,1,0:T(8,128)(2,1)S(1)} %get-tuple-element.33), channel_id=1, source_target_pairs={{0,3},{1,2},{2,1},{3,0},{4,7},{5,6},{6,5},{7,4},{8,11},{9,10},{10,... | collective-permute-start | bytes 122888 | tf_op jit(solution)/shard_map/ppermute | solution.py:429
  7.4 5.0 %collective-permute-start.2 = (bf16[2,80,128]{2,1,0:T(8,128)(2,1)S(1)}, bf16[2,80,128]{2,1,0:T(8,128)(2,1)S(1)}, u32[]{:S(2)}, u32[]{:S(2)}) collective-permute-start(bf16[2,80,128]{2,1,0:T(8,128)(2,1)S(1)} %get-tuple-element.34), channel_id=1, source_target_pairs={{0,1},{1,0},{2,3},{3,2},{4,5},{5,4},{6,7},{7,6},{8,9},{9,8},{10,11... | collective-permute-start | bytes 122888 | tf_op jit(solution)/shard_map/ppermute | solution.py:429
  7.6 11.5 %collective-permute-start.3 = (bf16[9,48,128]{2,1,0:T(8,128)(2,1)S(1)}, bf16[9,48,128]{2,1,0:T(8,128)(2,1)S(1)}, u32[]{:S(2)}, u32[]{:S(2)}) collective-permute-start(bf16[9,48,128]{2,1,0:T(8,128)(2,1)S(1)} %get-tuple-element.44), channel_id=1, source_target_pairs={{0,2},{1,3},{2,0},{3,1},{4,6},{5,7},{6,4},{7,5},{8,10},{9,11},{10,... | collective-permute-start | bytes 331784 | tf_op jit(solution)/shard_map/ppermute | solution.py:429
  10.4 8.7 %collective-permute-start.4 = (bf16[9,48,128]{2,1,0:T(8,128)(2,1)S(1)}, bf16[9,48,128]{2,1,0:T(8,128)(2,1)S(1)}, u32[]{:S(2)}, u32[]{:S(2)}) collective-permute-start(bf16[9,48,128]{2,1,0:T(8,128)(2,1)S(1)} %get-tuple-element.45), channel_id=1, source_target_pairs={{0,3},{1,2},{2,1},{3,0},{4,7},{5,6},{6,5},{7,4},{8,11},{9,10},{10,... | collective-permute-start | bytes 331784 | tf_op jit(solution)/shard_map/ppermute | solution.py:429
  11.8 7.6 %collective-permute-start.5 = (bf16[9,48,128]{2,1,0:T(8,128)(2,1)S(1)}, bf16[9,48,128]{2,1,0:T(8,128)(2,1)S(1)}, u32[]{:S(2)}, u32[]{:S(2)}) collective-permute-start(bf16[9,48,128]{2,1,0:T(8,128)(2,1)S(1)} %get-tuple-element.46), channel_id=1, source_target_pairs={{0,1},{1,0},{2,3},{3,2},{4,5},{5,4},{6,7},{7,6},{8,9},{9,8},{10,11... | collective-permute-start | bytes 331784 | tf_op jit(solution)/shard_map/ppermute | solution.py:429
  12.4 8.6 %collective-permute-start.6 = (bf16[4,80,128]{2,1,0:T(8,128)(2,1)S(1)}, bf16[4,80,128]{2,1,0:T(8,128)(2,1)S(1)}, u32[]{:S(2)}, u32[]{:S(2)}) collective-permute-start(bf16[4,80,128]{2,1,0:T(8,128)(2,1)S(1)} %get-tuple-element.49), channel_id=1, source_target_pairs={{0,4},{4,0},{8,12},{12,8},{16,20},{20,16},{24,28},{28,24},{1,5},{5... | collective-permute-start | bytes 245768 | tf_op jit(solution)/shard_map/ppermute | solution.py:429
  12.5 8.6 %collective-permute-start.7 = (bf16[4,80,128]{2,1,0:T(8,128)(2,1)S(1)}, bf16[4,80,128]{2,1,0:T(8,128)(2,1)S(1)}, u32[]{:S(2)}, u32[]{:S(2)}) collective-permute-start(bf16[4,80,128]{2,1,0:T(8,128)(2,1)S(1)} %get-tuple-element.50), channel_id=1, source_target_pairs={{4,8},{12,16},{20,24},{0,28},{8,4},{16,12},{24,20},{28,0},{5,9},{1... | collective-permute-start | bytes 245768 | tf_op jit(solution)/shard_map/ppermute | solution.py:504
  25.3 5.2 %collective-permute-start.8 = (bf16[2,128,128]{2,1,0:T(8,128)(2,1)S(1)}, bf16[2,128,128]{2,1,0:T(8,128)(2,1)S(1)}, u32[]{:S(2)}, u32[]{:S(2)}) collective-permute-start(bf16[2,128,128]{2,1,0:T(8,128)(2,1)S(1)} %get-tuple-element.56), channel_id=1, source_target_pairs={{0,24},{4,28},{8,16},{12,20},{16,8},{20,12},{24,0},{28,4},{1,25},{... | collective-permute-start | bytes 196616 | tf_op jit(solution)/shard_map/ppermute | solution.py:548
  27.9 4.3 %collective-permute-start.9 = (bf16[2,128,128]{2,1,0:T(8,128)(2,1)S(1)}, bf16[2,128,128]{2,1,0:T(8,128)(2,1)S(1)}, u32[]{:S(2)}, u32[]{:S(2)}) collective-permute-start(bf16[2,128,128]{2,1,0:T(8,128)(2,1)S(1)} %get-tuple-element.57), channel_id=1, source_target_pairs={{0,16},{4,12},{8,24},{12,4},{16,0},{20,28},{24,8},{28,20},{1,17},{... | collective-permute-start | bytes 196616 | tf_op jit(solution)/shard_map/ppermute | solution.py:548
  28.4 4.3 %collective-permute-start.10 = (bf16[2,128,128]{2,1,0:T(8,128)(2,1)S(1)}, bf16[2,128,128]{2,1,0:T(8,128)(2,1)S(1)}, u32[]{:S(2)}, u32[]{:S(2)}) collective-permute-start(bf16[2,128,128]{2,1,0:T(8,128)(2,1)S(1)} %get-tuple-element.58), channel_id=1, source_target_pairs={{0,8},{4,20},{8,0},{12,28},{16,24},{20,4},{24,16},{28,12},{1,9},{5... | collective-permute-start | bytes 196616 | tf_op jit(solution)/shard_map/ppermute | solution.py:548
  32.6 1.4 %collective-permute-start.11 = (bf16[4,128,128]{2,1,0:T(8,128)(2,1)S(1)}, bf16[4,128,128]{2,1,0:T(8,128)(2,1)S(1)}, u32[]{:S(2)}, u32[]{:S(2)}) collective-permute-start(bf16[4,128,128]{2,1,0:T(8,128)(2,1)S(1)} %get-tuple-element.60), channel_id=1, source_target_pairs={{0,4},{4,0},{8,12},{12,8},{16,20},{20,16},{24,28},{28,24},{1,5},{5... | collective-permute-start | bytes 393224 | tf_op jit(solution)/shard_map/ppermute | solution.py:429

commit v4 on v3

--- a/solution.py
+++ b/solution.py
@@ -505,6 +505,14 @@
     near = swap(near, "bulk", 1)
 
     whole = jax.ShapeDtypeStruct((2, planes_z, rows, LANES), F32)
+    border, target = pl.pallas_call(
+        lambda *refs: border_kernel(edge_order, *refs),
+        out_shape=[jax.ShapeDtypeStruct((2, planes_z, 2 * RADIUS, LANES), F32), targets],
+        in_specs=[vmem] * 6,
+        out_specs=[vmem] * 2,
+        input_output_aliases={0: 1},
+        compiler_params=params,
+    )(target, near, far, main_w, side_w, margin_w)
     fields, target = pl.pallas_call(
         lambda *refs: late_kernel(inner_order, *refs),
         out_shape=[whole, targets],
@@ -521,15 +529,6 @@
         side_w,
         inside_w,
     )
-    border, target = pl.pallas_call(
-        lambda *refs: border_kernel(edge_order, *refs),
-        out_shape=[jax.ShapeDtypeStruct((2, planes_z, 2 * RADIUS, LANES), F32), targets],
-        in_specs=[vmem] * 6,
-        out_specs=[vmem] * 2,
-        input_output_aliases={0: 1},
-        compiler_params=params,
-    )(target, near, far, main_w, side_w, margin_w)
-
     offers = jax.ShapeDtypeStruct((2, offered, LANES), BF16)
     _, dog, *chosen = pl.pallas_call(
         lambda *refs: filter_kernel(chips, *refs),

time: 35.5 us -> 34.6 us (0.975)
  waiting for transfers between devices: 7.8 us -> 6.91 us
    ppermute x8, waiting for transfers between devices: 4.06 us -> 2.4 us  [swap(): return lax.ppermute(block, axis, [(i, i ^ distance) for i in range(count)])]
    ppermute x1, waiting for transfers between devices: 0.01 us -> 0.77 us  [local(): far = lax.ppermute(far, 'bulk', far_pairs)]
  transfers between devices with their start and end apart: 12 -> 12, of which waited for: 7 -> 8; matrix products, arithmetic and copies ran while one was open for 0% -> 0% of each run, Pallas kernels for 11% -> 9%
where the time goes in v4:
time: 34.6 us; the launch traced here: 34.5 us
  starting transfers between devices  16.1 us (47%)
  Pallas kernels  9.7 us (28%)
  waiting for transfers between devices  6.91 us (20%)
  local copies, waits for them, and re-layouts  1.05 us (3%)
  between operations  0.75 us (2%)
    ppermute x8, starting transfers between devices, swap(): return lax.ppermute(block, axis, [(i, i ^ distance) for i in range(count)])  9.98 us
    ppermute x3, waiting for transfers between devices, local(): lax.ppermute(c, 'bulk', [(i, i ^ chip[i % 2]) for i in range(bricks)])  3.74 us
    ppermute x3, starting transfers between devices, local(): lax.ppermute(c, 'bulk', [(i, i ^ chip[i % 2]) for i in range(bricks)])  3.55 us
    pallas_call x1, Pallas kernels, local(): pl.pallas_call(lambda *refs: filter_kernel(chips, *refs), out_shape=[whol...  3.38 us
    ppermute x1, starting transfers between devices, local(): far = lax.ppermute(far, 'bulk', far_pairs)  2.55 us
    ppermute x8, waiting for transfers between devices, swap(): return lax.ppermute(block, axis, [(i, i ^ distance) for i in range(count)])  2.4 us
    pallas_call x1, Pallas kernels, local(): pl.pallas_call(lambda *refs: late_kernel(inner_order, *refs), out_shape=[...  1.6 us
    pallas_call x1, Pallas kernels, local(): pl.pallas_call(lambda *refs: finish_kernel(chips, *refs), out_shape=jax.S...  1.33 us
  transfers between devices with their start and end apart: 12, of which 8 were waited for; matrix products, arithmetic and copies ran while one was open for 0% of the time, Pallas kernels for 9%

profile of v4, /device:TPU:0, one launch (start us, length us, event | category | flops | bytes accessed | tf_op | source)
XLA Modules:
  0.0 34.5 jit_solution(8579984538238843642)
XLA Ops:
  0.6 0.0 copy-start
  0.6 1.0 %copy-done = bf16[8,64,512]{2,1,0:T(8,128)(2,1)S(1)} copy-done((bf16[8,64,512]{2,1,0:T(8,128)(2,1)S(1)}, bf16[8,64,512]{2,1,0:T(8,128)(2,1)}, u32[]{:S(2)}) %copy-start) | copy-done | bytes 524312
  1.7 0.0 copy-start.1
  1.7 0.0 copy-start.2
  1.7 0.0 copy-start.3
  1.7 0.3 shard_map.59
  2.0 4.1 %collective-permute-start = (bf16[2,80,128]{2,1,0:T(8,128)(2,1)S(1)}, bf16[2,80,128]{2,1,0:T(8,128)(2,1)S(1)}, u32[]{:S(2)}, u32[]{:S(2)}) collective-permute-start(bf16[2,80,128]{2,1,0:T(8,128)(2,1)S(1)} %get-tuple-element.32), channel_id=1, source_target_pairs={{0,2},{1,3},{2,0},{3,1},{4,6},{5,7},{6,4},{7,5},{8,10},{9,11},{10,... | collective-permute-start | bytes 122888 | tf_op jit(solution)/shard_map/ppermute | solution.py:429
  6.1 1.3 %collective-permute-start.1 = (bf16[2,80,128]{2,1,0:T(8,128)(2,1)S(1)}, bf16[2,80,128]{2,1,0:T(8,128)(2,1)S(1)}, u32[]{:S(2)}, u32[]{:S(2)}) collective-permute-start(bf16[2,80,128]{2,1,0:T(8,128)(2,1)S(1)} %get-tuple-element.33), channel_id=1, source_target_pairs={{0,3},{1,2},{2,1},{3,0},{4,7},{5,6},{6,5},{7,4},{8,11},{9,10},{10,... | collective-permute-start | bytes 122888 | tf_op jit(solution)/shard_map/ppermute | solution.py:429
  7.4 0.2 collective-permute-start.2
  7.6 2.8 %collective-permute-start.5 = (bf16[9,48,128]{2,1,0:T(8,128)(2,1)S(1)}, bf16[9,48,128]{2,1,0:T(8,128)(2,1)S(1)}, u32[]{:S(2)}, u32[]{:S(2)}) collective-permute-start(bf16[9,48,128]{2,1,0:T(8,128)(2,1)S(1)} %get-tuple-element.48), channel_id=1, source_target_pairs={{0,2},{1,3},{2,0},{3,1},{4,6},{5,7},{6,4},{7,5},{8,10},{9,11},{10,... | collective-permute-start | bytes 331784 | tf_op jit(solution)/shard_map/ppermute | solution.py:429
  10.4 1.3 %collective-permute-start.6 = (bf16[9,48,128]{2,1,0:T(8,128)(2,1)S(1)}, bf16[9,48,128]{2,1,0:T(8,128)(2,1)S(1)}, u32[]{:S(2)}, u32[]{:S(2)}) collective-permute-start(bf16[9,48,128]{2,1,0:T(8,128)(2,1)S(1)} %get-tuple-element.49), channel_id=1, source_target_pairs={{0,3},{1,2},{2,1},{3,0},{4,7},{5,6},{6,5},{7,4},{8,11},{9,10},{10,... | collective-permute-start | bytes 331784 | tf_op jit(solution)/shard_map/ppermute | solution.py:429
  11.8 0.0 collective-permute-done.refs_0_.refs_2_
  11.8 0.0 collective-permute-start.7
  11.8 0.6 %collective-permute-done.1.refs_1_.refs_3_ = bf16[2,80,128]{2,1,0:T(8,128)(2,1)S(1)} collective-permute-done((bf16[2,80,128]{2,1,0:T(8,128)(2,1)S(1)}, bf16[2,80,128]{2,1,0:T(8,128)(2,1)S(1)}, u32[]{:S(2)}, u32[]{:S(2)}) %collective-permute-start.1) | collective-permute-done | bytes 40992 | tf_op jit(solution)/shard_map/ppermute | solution.py:429
  12.4 0.0 collective-permute-done.2.refs_2_.refs_4_
  12.4 0.1 collective-permute-start.3
  12.5 2.5 %collective-permute-start.4 = (bf16[4,80,128]{2,1,0:T(8,128)(2,1)S(1)}, bf16[4,80,128]{2,1,0:T(8,128)(2,1)S(1)}, u32[]{:S(2)}, u32[]{:S(2)}) collective-permute-start(bf16[4,80,128]{2,1,0:T(8,128)(2,1)S(1)} %get-tuple-element.44), channel_id=1, source_target_pairs={{4,8},{12,16},{20,24},{0,28},{8,4},{16,12},{24,20},{28,0},{5,9},{1... | collective-permute-start | bytes 245768 | tf_op jit(solution)/shard_map/ppermute | solution.py:504
  15.0 0.5 %shard_map.61 = (bf16[256,256]{1,0:T(8,128)(2,1)S(1)}, bf16[8,256,256]{2,1,0:T(8,128)(2,1)S(1)}, bf16[2,64,256]{2,1,0:T(8,128)(2,1)S(1)}, bf16[2,64,256]{2,1,0:T(8,128)(2,1)S(1)}) custom-call(bf16[2,80,128]{2,1,0:T(8,128)(2,1)S(1)} %get-tuple-element.35.refs_3_.packed_ref.edge_ref), custom_call_target="tpu_custom_call" | custom-call | tf_op jit(solution)/shard_map/pallas_call | solution.py:462
  15.5 1.1 %shard_map.62 = (f32[2,8,64,128]{3,2,1,0:T(8,128)S(1)}, f32[8,128]{1,0:T(8,128)S(1)}) custom-call(f32[8,128]{1,0:T(8,128)S(1)} %get-tuple-element.36.token_ref, bf16[2,80,128]{2,1,0:T(8,128)(2,1)S(1)} %get-tuple-element.35.refs_3_.packed_ref.edge_ref, bf16[9,48,128]{2,1,0:T(8,128)(2,1)S(1)} %get-tuple-element.37.inner_ref, ...), custom_call_target="tpu_custom_call", output_to_operand_aliasing={{1}: (0, {})} | custom-call | tf_op jit(solution)/shard_map/pallas_call | solution.py:482
  16.7 0.0 copy-done.1
  16.7 0.0 copy-done.2
  16.7 0.0 copy-done.3
  16.7 0.1 shard_map.63
  16.8 0.0 collective-permute-done.3.refs_1_
  16.8 0.8 %collective-permute-done.4.refs_2_ = bf16[4,80,128]{2,1,0:T(8,128)(2,1)S(1)} collective-permute-done((bf16[4,80,128]{2,1,0:T(8,128)(2,1)S(1)}, bf16[4,80,128]{2,1,0:T(8,128)(2,1)S(1)}, u32[]{:S(2)}, u32[]{:S(2)}) %collective-permute-start.4) | collective-permute-done | bytes 81952 | tf_op jit(solution)/shard_map/ppermute | solution.py:504
  17.6 0.9 %shard_map.64 = (f32[2,32,16,128]{3,2,1,0:T(8,128)S(1)}, s32[8,128]{1,0:T(8,128)S(1)}) custom-call(s32[8,128]{1,0:T(8,128)S(1)} %get-tuple-element.42.refs_0_, bf16[4,80,128]{2,1,0:T(8,128)(2,1)S(1)} %collective-permute-done.3.refs_1_, bf16[4,80,128]{2,1,0:T(8,128)(2,1)S(1)} %collective-permute-done.4.refs_2_, ...), custom_call_target="tpu_custom_call", output_to_operand_aliasing={{1}: (0, {})} | custom-call | tf_op jit(solution)/shard_map/pallas_call | solution.py:508
  18.5 0.6 %collective-permute-done.5.refs_5_ = bf16[9,48,128]{2,1,0:T(8,128)(2,1)S(1)} collective-permute-done((bf16[9,48,128]{2,1,0:T(8,128)(2,1)S(1)}, bf16[9,48,128]{2,1,0:T(8,128)(2,1)S(1)}, u32[]{:S(2)}, u32[]{:S(2)}) %collective-permute-start.5) | collective-permute-done | bytes 110624 | tf_op jit(solution)/shard_map/ppermute | solution.py:429
  19.1 0.0 collective-permute-done.6.refs_6_
  19.1 0.3 collective-permute-done.7.refs_7_
  19.4 1.6 %shard_map.65 = (f32[2,32,64,128]{3,2,1,0:T(8,128)S(1)}, s32[8,128]{1,0:T(8,128)S(1)}) custom-call(s32[8,128]{1,0:T(8,128)S(1)} %get-tuple-element.46.refs_0_, f32[2,8,64,128]{3,2,1,0:T(8,128)S(1)} %get-tuple-element.47.refs_1_, bf16[2,80,128]{2,1,0:T(8,128)(2,1)S(1)} %collective-permute-done.refs_0_.refs_2_, ...), custom_call_target="tpu_custom_call", output_to_operand_aliasing={{1}: (0, {})} | custom-call | tf_op jit(solution)/shard_map/pallas_call | solution.py:516
  21.0 3.4 %shard_map.66 = (f32[2,32,64,128]{3,2,1,0:T(8,128)S(1)}, bf16[32,64,128]{2,1,0:T(8,128)(2,1)}, bf16[2,128,128]{2,1,0:T(8,128)(2,1)S(1)}, bf16[2,128,128]{2,1,0:T...) custom-call(f32[2,32,64,128]{3,2,1,0:T(8,128)S(1)} %get-tuple-elemen, ...), custom_call_target="tpu_custom_call", output_to_operand_aliasing={{0}: (0, {})} | custom-call | tf_op jit(solution)/shard_map/pallas_call | solution.py:533
  24.4 2.5 %collective-permute-start.8 = (bf16[2,128,128]{2,1,0:T(8,128)(2,1)S(1)}, bf16[2,128,128]{2,1,0:T(8,128)(2,1)S(1)}, u32[]{:S(2)}, u32[]{:S(2)}) collective-permute-start(bf16[2,128,128]{2,1,0:T(8,128)(2,1)S(1)} %get-tuple-element.56), channel_id=1, source_target_pairs={{0,24},{4,28},{8,16},{12,20},{16,8},{20,12},{24,0},{28,4},{1,25},{... | collective-permute-start | bytes 196616 | tf_op jit(solution)/shard_map/ppermute | solution.py:547
  26.9 0.5 %collective-permute-start.9 = (bf16[2,128,128]{2,1,0:T(8,128)(2,1)S(1)}, bf16[2,128,128]{2,1,0:T(8,128)(2,1)S(1)}, u32[]{:S(2)}, u32[]{:S(2)}) collective-permute-start(bf16[2,128,128]{2,1,0:T(8,128)(2,1)S(1)} %get-tuple-element.57), channel_id=1, source_target_pairs={{0,16},{4,12},{8,24},{12,4},{16,0},{20,28},{24,8},{28,20},{1,17},{... | collective-permute-start | bytes 196616 | tf_op jit(solution)/shard_map/ppermute | solution.py:547
  27.5 0.5 %collective-permute-start.10 = (bf16[2,128,128]{2,1,0:T(8,128)(2,1)S(1)}, bf16[2,128,128]{2,1,0:T(8,128)(2,1)S(1)}, u32[]{:S(2)}, u32[]{:S(2)}) collective-permute-start(bf16[2,128,128]{2,1,0:T(8,128)(2,1)S(1)} %get-tuple-element.58), channel_id=1, source_target_pairs={{0,8},{4,20},{8,0},{12,28},{16,24},{20,4},{24,16},{28,12},{1,9},{5... | collective-permute-start | bytes 196616 | tf_op jit(solution)/shard_map/ppermute | solution.py:547
  28.0 2.3 %collective-permute-done.8.refs_0_.refs_1_ = bf16[2,128,128]{2,1,0:T(8,128)(2,1)S(1)} collective-permute-done((bf16[2,128,128]{2,1,0:T(8,128)(2,1)S(1)}, bf16[2,128,128]{2,1,0:T(8,128)(2,1)S(1)}, u32[]{:S(2)}, u32[]{:S(2)}) %collective-permute-start.8) | collective-permute-done | bytes 65568 | tf_op jit(solution)/shard_map/ppermute | solution.py:547
  30.3 0.9 %collective-permute-done.9.refs_1_.refs_2_ = bf16[2,128,128]{2,1,0:T(8,128)(2,1)S(1)} collective-permute-done((bf16[2,128,128]{2,1,0:T(8,128)(2,1)S(1)}, bf16[2,128,128]{2,1,0:T(8,128)(2,1)S(1)}, u32[]{:S(2)}, u32[]{:S(2)}) %collective-permute-start.9) | collective-permute-done | bytes 65568 | tf_op jit(solution)/shard_map/ppermute | solution.py:547
  31.2 0.5 %collective-permute-done.10.refs_2_.refs_3_ = bf16[2,128,128]{2,1,0:T(8,128)(2,1)S(1)} collective-permute-done((bf16[2,128,128]{2,1,0:T(8,128)(2,1)S(1)}, bf16[2,128,128]{2,1,0:T(8,128)(2,1)S(1)}, u32[]{:S(2)}, u32[]{:S(2)}) %collective-permute-start.10) | collective-permute-done | bytes 65568 | tf_op jit(solution)/shard_map/ppermute | solution.py:547
  31.7 0.1 collective-permute-start.11
  31.8 0.5 %shard_map.68.refs_2_ = f32[1024,128]{1,0:T(8,128)S(1)} custom-call(s32[8,128]{1,0:T(8,128)S(1)} %get-tuple-element.61.refs_0_.refs_1_, bf16[2,128,128]{2,1,0:T(8,128)(2,1)S(1)} %collective-permute-done.8.refs_0_.refs_1_, bf16[2,128,128]{2,1,0:T(8,128)(2,1)S(1)} %collective-permute-done.9.refs_1_.refs_2_, ...), custom_call_target="tpu_custom_call" | custom-call | tf_op jit(solution)/shard_map/pallas_call | solution.py:559
  32.3 0.8 %collective-permute-done.11.refs_0_ = bf16[4,128,128]{2,1,0:T(8,128)(2,1)S(1)} collective-permute-done((bf16[4,128,128]{2,1,0:T(8,128)(2,1)S(1)}, bf16[4,128,128]{2,1,0:T(8,128)(2,1)S(1)}, u32[]{:S(2)}, u32[]{:S(2)}) %collective-permute-start.11) | collective-permute-done | bytes 131104 | tf_op jit(solution)/shard_map/ppermute | solution.py:429
  33.2 1.3 %shard_map.69 = f32[1024,128]{1,0:T(8,128)} custom-call(bf16[4,128,128]{2,1,0:T(8,128)(2,1)S(1)} %collective-permute-done.11.refs_0_, s32[8,128]{1,0:T(8,128)S(1)} %get-tuple-element.61.refs_0_.refs_1_, f32[1024,128]{1,0:T(8,128)S(1)} %shard_map.68.refs_2_), custom_call_target="tpu_custom_call" | custom-call | tf_op jit(solution)/shard_map/pallas_call | solution.py:566
  (2 shorter events, 0.0 us)
Async XLA Ops:
  0.6 1.0 %copy-start = (bf16[8,64,512]{2,1,0:T(8,128)(2,1)S(1)}, bf16[8,64,512]{2,1,0:T(8,128)(2,1)}, u32[]{:S(2)}) copy-start(bf16[8,64,512]{2,1,0:T(8,128)(2,1)} %refs_0_.1) | copy-start | bytes 1572868
  1.7 15.0 %copy-start.1 = (s32[1,1,8,128]{3,2,1,0:T(8,128)S(1)}, s32[1,1,8,128]{3,2,1,0:T(8,128)}, u32[]{:S(2)}) copy-start(s32[1,1,8,128]{3,2,1,0:T(8,128)} %param.5) | copy-start | bytes 12292
  1.7 15.0 %copy-start.2 = (s32[1,1,8,128]{3,2,1,0:T(8,128)S(1)}, s32[1,1,8,128]{3,2,1,0:T(8,128)}, u32[]{:S(2)}) copy-start(s32[1,1,8,128]{3,2,1,0:T(8,128)} %param.6) | copy-start | bytes 12292
  1.7 15.0 %copy-start.3 = (s32[1,1,8]{2,1,0:T(1,128)S(1)}, s32[1,1,8]{2,1,0:T(1,128)}, u32[]{:S(2)}) copy-start(s32[1,1,8]{2,1,0:T(1,128)} %param.7) | copy-start | bytes 100
  2.0 9.8 %collective-permute-start = (bf16[2,80,128]{2,1,0:T(8,128)(2,1)S(1)}, bf16[2,80,128]{2,1,0:T(8,128)(2,1)S(1)}, u32[]{:S(2)}, u32[]{:S(2)}) collective-permute-start(bf16[2,80,128]{2,1,0:T(8,128)(2,1)S(1)} %get-tuple-element.32), channel_id=1, source_target_pairs={{0,2},{1,3},{2,0},{3,1},{4,6},{5,7},{6,4},{7,5},{8,10},{9,11},{10,... | collective-permute-start | bytes 122888 | tf_op jit(solution)/shard_map/ppermute | solution.py:429
  6.1 6.3 %collective-permute-start.1 = (bf16[2,80,128]{2,1,0:T(8,128)(2,1)S(1)}, bf16[2,80,128]{2,1,0:T(8,128)(2,1)S(1)}, u32[]{:S(2)}, u32[]{:S(2)}) collective-permute-start(bf16[2,80,128]{2,1,0:T(8,128)(2,1)S(1)} %get-tuple-element.33), channel_id=1, source_target_pairs={{0,3},{1,2},{2,1},{3,0},{4,7},{5,6},{6,5},{7,4},{8,11},{9,10},{10,... | collective-permute-start | bytes 122888 | tf_op jit(solution)/shard_map/ppermute | solution.py:429
  7.4 5.0 %collective-permute-start.2 = (bf16[2,80,128]{2,1,0:T(8,128)(2,1)S(1)}, bf16[2,80,128]{2,1,0:T(8,128)(2,1)S(1)}, u32[]{:S(2)}, u32[]{:S(2)}) collective-permute-start(bf16[2,80,128]{2,1,0:T(8,128)(2,1)S(1)} %get-tuple-element.34), channel_id=1, source_target_pairs={{0,1},{1,0},{2,3},{3,2},{4,5},{5,4},{6,7},{7,6},{8,9},{9,8},{10,11... | collective-permute-start | bytes 122888 | tf_op jit(solution)/shard_map/ppermute | solution.py:429
  7.6 11.5 %collective-permute-start.5 = (bf16[9,48,128]{2,1,0:T(8,128)(2,1)S(1)}, bf16[9,48,128]{2,1,0:T(8,128)(2,1)S(1)}, u32[]{:S(2)}, u32[]{:S(2)}) collective-permute-start(bf16[9,48,128]{2,1,0:T(8,128)(2,1)S(1)} %get-tuple-element.48), channel_id=1, source_target_pairs={{0,2},{1,3},{2,0},{3,1},{4,6},{5,7},{6,4},{7,5},{8,10},{9,11},{10,... | collective-permute-start | bytes 331784 | tf_op jit(solution)/shard_map/ppermute | solution.py:429
  10.4 8.7 %collective-permute-start.6 = (bf16[9,48,128]{2,1,0:T(8,128)(2,1)S(1)}, bf16[9,48,128]{2,1,0:T(8,128)(2,1)S(1)}, u32[]{:S(2)}, u32[]{:S(2)}) collective-permute-start(bf16[9,48,128]{2,1,0:T(8,128)(2,1)S(1)} %get-tuple-element.49), channel_id=1, source_target_pairs={{0,3},{1,2},{2,1},{3,0},{4,7},{5,6},{6,5},{7,4},{8,11},{9,10},{10,... | collective-permute-start | bytes 331784 | tf_op jit(solution)/shard_map/ppermute | solution.py:429
  11.8 7.6 %collective-permute-start.7 = (bf16[9,48,128]{2,1,0:T(8,128)(2,1)S(1)}, bf16[9,48,128]{2,1,0:T(8,128)(2,1)S(1)}, u32[]{:S(2)}, u32[]{:S(2)}) collective-permute-start(bf16[9,48,128]{2,1,0:T(8,128)(2,1)S(1)} %get-tuple-element.50), channel_id=1, source_target_pairs={{0,1},{1,0},{2,3},{3,2},{4,5},{5,4},{6,7},{7,6},{8,9},{9,8},{10,11... | collective-permute-start | bytes 331784 | tf_op jit(solution)/shard_map/ppermute | solution.py:429
  12.4 4.4 %collective-permute-start.3 = (bf16[4,80,128]{2,1,0:T(8,128)(2,1)S(1)}, bf16[4,80,128]{2,1,0:T(8,128)(2,1)S(1)}, u32[]{:S(2)}, u32[]{:S(2)}) collective-permute-start(bf16[4,80,128]{2,1,0:T(8,128)(2,1)S(1)} %get-tuple-element.43), channel_id=1, source_target_pairs={{0,4},{4,0},{8,12},{12,8},{16,20},{20,16},{24,28},{28,24},{1,5},{5... | collective-permute-start | bytes 245768 | tf_op jit(solution)/shard_map/ppermute | solution.py:429
  12.5 5.1 %collective-permute-start.4 = (bf16[4,80,128]{2,1,0:T(8,128)(2,1)S(1)}, bf16[4,80,128]{2,1,0:T(8,128)(2,1)S(1)}, u32[]{:S(2)}, u32[]{:S(2)}) collective-permute-start(bf16[4,80,128]{2,1,0:T(8,128)(2,1)S(1)} %get-tuple-element.44), channel_id=1, source_target_pairs={{4,8},{12,16},{20,24},{0,28},{8,4},{16,12},{24,20},{28,0},{5,9},{1... | collective-permute-start | bytes 245768 | tf_op jit(solution)/shard_map/ppermute | solution.py:504
  24.4 5.8 %collective-permute-start.8 = (bf16[2,128,128]{2,1,0:T(8,128)(2,1)S(1)}, bf16[2,128,128]{2,1,0:T(8,128)(2,1)S(1)}, u32[]{:S(2)}, u32[]{:S(2)}) collective-permute-start(bf16[2,128,128]{2,1,0:T(8,128)(2,1)S(1)} %get-tuple-element.56), channel_id=1, source_target_pairs={{0,24},{4,28},{8,16},{12,20},{16,8},{20,12},{24,0},{28,4},{1,25},{... | collective-permute-start | bytes 196616 | tf_op jit(solution)/shard_map/ppermute | solution.py:547
  26.9 4.3 %collective-permute-start.9 = (bf16[2,128,128]{2,1,0:T(8,128)(2,1)S(1)}, bf16[2,128,128]{2,1,0:T(8,128)(2,1)S(1)}, u32[]{:S(2)}, u32[]{:S(2)}) collective-permute-start(bf16[2,128,128]{2,1,0:T(8,128)(2,1)S(1)} %get-tuple-element.57), channel_id=1, source_target_pairs={{0,16},{4,12},{8,24},{12,4},{16,0},{20,28},{24,8},{28,20},{1,17},{... | collective-permute-start | bytes 196616 | tf_op jit(solution)/shard_map/ppermute | solution.py:547
  27.5 4.3 %collective-permute-start.10 = (bf16[2,128,128]{2,1,0:T(8,128)(2,1)S(1)}, bf16[2,128,128]{2,1,0:T(8,128)(2,1)S(1)}, u32[]{:S(2)}, u32[]{:S(2)}) collective-permute-start(bf16[2,128,128]{2,1,0:T(8,128)(2,1)S(1)} %get-tuple-element.58), channel_id=1, source_target_pairs={{0,8},{4,20},{8,0},{12,28},{16,24},{20,4},{24,16},{28,12},{1,9},{5... | collective-permute-start | bytes 196616 | tf_op jit(solution)/shard_map/ppermute | solution.py:547
  31.7 1.4 %collective-permute-start.11 = (bf16[4,128,128]{2,1,0:T(8,128)(2,1)S(1)}, bf16[4,128,128]{2,1,0:T(8,128)(2,1)S(1)}, u32[]{:S(2)}, u32[]{:S(2)}) collective-permute-start(bf16[4,128,128]{2,1,0:T(8,128)(2,1)S(1)} %get-tuple-element.60), channel_id=1, source_target_pairs={{0,4},{4,0},{8,12},{12,8},{16,20},{20,16},{24,28},{28,24},{1,5},{5... | collective-permute-start | bytes 393224 | tf_op jit(solution)/shard_map/ppermute | solution.py:429
